TPU v7x, 512 devices: a whole 4x4x16 slice. The times are simulated.
512 devices in a mesh: loop: 64 (over y_hi, z, core), grp: 8 (over x, y_lo).
Axes of the slice: x: 4, y: 4 (y_hi: 2, y_lo: 2; y = y_hi * 2 + y_lo), z: 16, core: 2. Of those that a mesh axis runs over, the one named last changes fastest.
Arguments:
- student: bfloat16 [65536, 1024], P('loop', 'grp'), may hold values from -0.75 to 0.75
- teacher_tiles: bfloat16 [65536, 4, 1024], P(('loop', 'grp')), may hold values from -0.59765625 to 0.59765625
Outputs:
- student_grad: float32 [65536, 1024], P('loop', 'grp')
All inputs are finite; a program needn't handle non-finite values.
Results may differ from a plain program's by a relative error of at most 0.0052.
Values may be sent and summed in bfloat16 or wider, within the bound.
A program may use at most 64 MiB of HBM per device.

v0:
```python
import jax
import jax.numpy as jnp
from jax import lax
from jax.sharding import PartitionSpec as P

STEPS = 4


def passed_along(block, axis, distance):
    devices = range(lax.axis_size(axis))
    route = [((i - distance) % len(devices), i) for i in devices]
    return lax.ppermute(block, axis, route)


def per_device(student, teacher_tiles):
    rows = student.shape[0]
    width = student.shape[1]
    member = lax.axis_index("grp")
    values = student.astype(jnp.float32)
    squares = lax.psum(jnp.sum(values * values, axis=1), "grp")
    norms = jnp.sqrt(squares + 1e-06)
    unit = values / norms[:, None]
    unit_bf = unit.astype(jnp.bfloat16)
    home_block = lax.all_to_all(unit_bf, "grp", split_axis=0, concat_axis=1, tiled=True)
    own_grad = jnp.zeros((rows, width), jnp.float32)
    far_terms = []
    visitor_full = lax.all_gather(unit_bf, "grp", axis=1, tiled=True)
    for step in range(STEPS):
        if step > 0:
            visitor_full = passed_along(visitor_full, "loop", 1)
        visitor_part = lax.dynamic_slice_in_dim(visitor_full, member * width, width, 1)
        similar = lax.dot_general(
            home_block, visitor_full, (((1,), (1,)), ((), ())), preferred_element_type=jnp.float32
        )
        errors = (similar - teacher_tiles[:, step, :].astype(jnp.float32)).astype(jnp.bfloat16)
        errors_all = lax.all_gather(errors, "grp", axis=0, tiled=True)
        own_grad = own_grad + jnp.dot(errors_all, visitor_part, preferred_element_type=jnp.float32)
        far_terms.append(
            lax.dot_general(
                errors_all, unit_bf, (((0,), (0,)), ((), ())), preferred_element_type=jnp.float32
            )
        )
    carried = far_terms[STEPS - 1]
    for step in range(STEPS - 1, 0, -1):
        carried = passed_along(carried, "loop", -1) + far_terms[step - 1]
    unit_grad = 2.0 * own_grad + 2.0 * carried
    inner = lax.psum(jnp.sum(unit * unit_grad, axis=1), "grp")
    return (unit_grad - unit * inner[:, None]) / norms[:, None]


def solution(mesh):
    placed = (P("loop", "grp"), P(("loop", "grp"), None, None))
    return jax.shard_map(
        per_device, mesh=mesh, in_specs=placed, out_specs=P("loop", "grp"), check_vma=False
    )
```

profile of v0, /device:TPU:1, one launch (start us, length us, event | category | flops | bytes accessed | tf_op | source)
XLA Modules:
  0.0 461.0 jit_solution(13023876328428725749)
XLA Ops:
  6.5 0.0 all-gather.6.cloned.1.call-start
  6.5 1.2 copy.12
  7.7 0.1 fusion.6
  7.8 16.8 %psum.14 = f32[1024]{0:T(1024)S(1)} all-reduce(f32[1024]{0:T(1024)S(1)} %fusion.6), channel_id=1, replica_groups=mesh['loop'=64,'grp'=8] {'grp'}, use_global_device_ids=true, to_apply=%region_1.0 | all-reduce | flops 1024 | bytes 8192 | tf_op jit(solution)/shard_map/psum | solution.py:20
  24.6 0.8 fusion.12
  25.4 0.0 all-gather.6.cloned.1.call-update
  25.4 63.3 %all-gather.6.cloned.1.call-done = bf16[1024,1024]{0,1:T(8,128)(2,1)} async-done(((bf16[1024,128]{0,1:T(8,128)(2,1)}), bf16[1024,1024]{0,1:T(8,128)(2,1)}) %all-gather.6.cloned.1.call-update) | async-done | bytes 2097168 | tf_op jit(solution)/shard_map/all_gather | solution.py:27
  88.7 4.5 collective-permute-start
  93.2 23.3 %collective-permute-done = bf16[1024,1024]{0,1:T(8,128)(2,1)S(1)} collective-permute-done((bf16[1024,1024]{0,1:T(8,128)(2,1)}, bf16[1024,1024]{0,1:T(8,128)(2,1)S(1)}, u32[]{:S(2)}, u32[]{:S(2)}) %collective-permute-start) | collective-permute-done | bytes 2097184 | tf_op jit(solution)/shard_map/ppermute | solution.py:12
  116.5 1.3 copy-done.5
  117.8 4.3 collective-permute-start.1
  122.1 23.0 %collective-permute-done.1 = bf16[1024,1024]{0,1:T(8,128)(2,1)} collective-permute-done((bf16[1024,1024]{0,1:T(8,128)(2,1)S(1)}, bf16[1024,1024]{0,1:T(8,128)(2,1)}, u32[]{:S(2)}, u32[]{:S(2)}) %collective-permute-start.1) | collective-permute-done | bytes 2097184 | tf_op jit(solution)/shard_map/ppermute | solution.py:12
  145.1 4.5 collective-permute-start.2
  149.6 0.8 copy_bitcast_fusion
  150.3 4.5 all-to-all-start
  154.8 0.0 all-gather.14.cloned.1.call-start
  154.8 0.0 copy-done.4
  154.8 2.5 fusion.17
  157.3 3.2 all-to-all-done
  160.6 12.3 %collective-permute-done.2 = bf16[1024,1024]{0,1:T(8,128)(2,1)} collective-permute-done((bf16[1024,1024]{0,1:T(8,128)(2,1)}, bf16[1024,1024]{0,1:T(8,128)(2,1)}, u32[]{:S(2)}, u32[]{:S(2)}) %collective-permute-start.2) | collective-permute-done | bytes 2097184 | tf_op jit(solution)/shard_map/ppermute | solution.py:12
  172.8 2.9 fusion.5
  175.7 0.0 all-gather.14.cloned.1.call-update
  175.7 0.0 all-gather.8.cloned.1.call-start
  175.8 0.0 copy-done.7
  175.8 2.2 fusion.2
  178.0 0.0 all-gather.8.cloned.1.call-update
  178.0 0.0 all-gather.12.cloned.1.call-start
  178.1 3.0 fusion.4
  181.0 0.0 all-gather.12.cloned.1.call-update
  181.1 0.0 all-gather.10.cloned.1.call-start
  181.1 0.0 copy-done.6
  181.1 1.2 fusion.3
  182.3 0.0 all-gather.10.cloned.1.call-update
  182.3 56.1 %all-gather.14.cloned.1.call-done = bf16[1024,1024]{1,0:T(8,128)(2,1)} async-done(((bf16[128,1024]{1,0:T(8,128)(2,1)}), bf16[1024,1024]{1,0:T(8,128)(2,1)}) %all-gather.14.cloned.1.call-update) | async-done | bytes 2097168 | tf_op jit(solution)/shard_map/all_gather | solution.py:36
  238.5 0.0 copy-done.2
  238.5 2.8 fusion.18
  241.3 3.8 collective-permute-start.3
  245.2 54.5 %all-gather.8.cloned.1.call-done = bf16[1024,1024]{1,0:T(8,128)(2,1)} async-done(((bf16[128,1024]{1,0:T(8,128)(2,1)}), bf16[1024,1024]{1,0:T(8,128)(2,1)}) %all-gather.8.cloned.1.call-update) | async-done | bytes 2097168 | tf_op jit(solution)/shard_map/all_gather | solution.py:36
  299.7 2.8 fusion.20
  302.5 58.2 %all-gather.12.cloned.1.call-done = bf16[1024,1024]{1,0:T(8,128)(2,1)} async-done(((bf16[128,1024]{1,0:T(8,128)(2,1)}), bf16[1024,1024]{1,0:T(8,128)(2,1)}) %all-gather.12.cloned.1.call-update) | async-done | bytes 2097168 | tf_op jit(solution)/shard_map/all_gather | solution.py:36
  360.8 0.0 collective-permute-done.3
  360.8 2.8 convolution_add_fusion
  363.6 3.9 collective-permute-start.4
  367.5 0.0 copy-done.3
  367.5 1.8 fusion.10
  369.3 52.6 %all-gather.10.cloned.1.call-done = bf16[1024,1024]{1,0:T(8,128)(2,1)} async-done(((bf16[128,1024]{1,0:T(8,128)(2,1)}), bf16[1024,1024]{1,0:T(8,128)(2,1)}) %all-gather.10.cloned.1.call-update) | async-done | bytes 2097168 | tf_op jit(solution)/shard_map/all_gather | solution.py:36
  421.9 2.2 fusion.19
  424.0 0.0 collective-permute-done.4
  424.1 1.1 add.45
  425.2 0.0 copy-start.1
  425.2 4.0 collective-permute-start.5
  429.2 0.0 copy-done
  429.2 1.8 convolution_add_fusion.3
  431.0 0.0 copy-done.1
  431.0 0.0 copy-start.8
  431.0 0.0 copy-start.9
  431.0 1.9 convolution_add_fusion.2
  432.9 3.7 collective-permute-done.5
  436.7 0.0 copy-done.8
  436.7 0.0 copy-done.9
  436.7 1.8 multiply_reduce_fusion
  438.5 14.8 %psum.15 = f32[1024]{0:T(1024)S(1)} all-reduce(f32[1024]{0:T(1024)S(1)} %get-tuple-element.9), channel_id=1, replica_groups=mesh['loop'=64,'grp'=8] {'grp'}, use_global_device_ids=true, to_apply=%region_3.0 | all-reduce | flops 1024 | bytes 8192 | tf_op jit(solution)/shard_map/psum | solution.py:47
  453.4 0.1 subtract_divide_fusion
  453.5 1.0 copy.21
  (8 shorter events, 0.0 us)
Async XLA Ops:
  6.5 148.3 %copy-start.4 = (bf16[128,4,1024]{2,1,0:T(4,128)(2,1)S(1)}, bf16[128,4,1024]{2,1,0:T(4,128)(2,1)}, u32[]{:S(2)}) copy-start(bf16[128,4,1024]{2,1,0:T(4,128)(2,1)} %param.3) | copy-start | bytes 3145732
  6.5 82.1 %all-gather.6.cloned.1.call-start = ((), (), s32[]{:S(2)}) async-start(), calls=%async_computation.1 | async-start | bytes 2359296 | tf_op jit(solution)/shard_map/all_gather | solution.py:27
  88.7 27.8 %collective-permute-start = (bf16[1024,1024]{0,1:T(8,128)(2,1)}, bf16[1024,1024]{0,1:T(8,128)(2,1)S(1)}, u32[]{:S(2)}, u32[]{:S(2)}) collective-permute-start(bf16[1024,1024]{0,1:T(8,128)(2,1)} %all-gather.6.cloned.1.call-done), channel_id=1, source_target_pairs={{504,0},{0,8},{8,16},{16,24},{24,32},{32,40},{40,48},{48,56},{56,6... | collective-permute-start | bytes 6291464 | tf_op jit(solution)/shard_map/ppermute | solution.py:12
  116.5 1.3 copy-start.5
  117.8 27.2 %collective-permute-start.1 = (bf16[1024,1024]{0,1:T(8,128)(2,1)S(1)}, bf16[1024,1024]{0,1:T(8,128)(2,1)}, u32[]{:S(2)}, u32[]{:S(2)}) collective-permute-start(bf16[1024,1024]{0,1:T(8,128)(2,1)S(1)} %collective-permute-done), channel_id=1, source_target_pairs={{504,0},{0,8},{8,16},{16,24},{24,32},{32,40},{40,48},{48,56},{56,6... | collective-permute-start | bytes 6291464 | tf_op jit(solution)/shard_map/ppermute | solution.py:12
  145.1 27.8 %collective-permute-start.2 = (bf16[1024,1024]{0,1:T(8,128)(2,1)}, bf16[1024,1024]{0,1:T(8,128)(2,1)}, u32[]{:S(2)}, u32[]{:S(2)}) collective-permute-start(bf16[1024,1024]{0,1:T(8,128)(2,1)} %collective-permute-done.1), channel_id=1, source_target_pairs={{504,0},{0,8},{8,16},{16,24},{24,32},{32,40},{40,48},{48,56},{56,6... | collective-permute-start | bytes 6291464 | tf_op jit(solution)/shard_map/ppermute | solution.py:12
  150.3 10.2 %all-to-all-start = ((bf16[8,128,128]{1,2,0:T(8,128)(2,1)}), bf16[8,128,128]{1,2,0:T(8,128)(2,1)S(1)}, u32[]{:S(2)}, u32[]{:S(2)}) async-start(bf16[8,128,128]{1,2,0:T(8,128)(2,1)} %copy_bitcast_fusion), calls=%async_computation | async-start | bytes 524288 | tf_op jit(solution)/shard_map/all_to_all | solution.py:24
  154.8 83.7 %all-gather.14.cloned.1.call-start = ((), (), s32[]{:S(2)}) async-start(), calls=%async_computation.5 | async-start | bytes 2359296 | tf_op jit(solution)/shard_map/all_gather | solution.py:36
  157.3 18.4 %copy-start.7 = (bf16[1024,1024]{0,1:T(8,128)(2,1)S(1)}, bf16[1024,1024]{0,1:T(8,128)(2,1)}, u32[]{:S(2)}) copy-start(bf16[1024,1024]{0,1:T(8,128)(2,1)} %all-gather.6.cloned.1.call-done) | copy-start | bytes 6291460
  175.7 124.0 %all-gather.8.cloned.1.call-start = ((), (), s32[]{:S(2)}) async-start(), calls=%async_computation.2 | async-start | bytes 2359296 | tf_op jit(solution)/shard_map/all_gather | solution.py:36
  178.0 3.1 copy-start.6
  178.0 182.8 %all-gather.12.cloned.1.call-start = ((), (), s32[]{:S(2)}) async-start(), calls=%async_computation.4 | async-start | bytes 2359296 | tf_op jit(solution)/shard_map/all_gather | solution.py:36
  181.0 57.4 %copy-start.2 = (bf16[1024,128]{0,1:T(8,128)(2,1)S(1)}, bf16[1024,128]{0,1:T(8,128)(2,1)}, u32[]{:S(2)}) copy-start(bf16[1024,128]{0,1:T(8,128)(2,1)} %fusion.12) | copy-start | bytes 786436
  181.1 240.8 %all-gather.10.cloned.1.call-start = ((), (), s32[]{:S(2)}) async-start(), calls=%async_computation.3 | async-start | bytes 2359296 | tf_op jit(solution)/shard_map/all_gather | solution.py:36
  241.3 119.5 %collective-permute-start.3 = (f32[1024,128]{0,1:T(8,128)}, f32[1024,128]{0,1:T(8,128)S(1)}, u32[]{:S(2)}, u32[]{:S(2)}) collective-permute-start(f32[1024,128]{0,1:T(8,128)} %fusion.18), channel_id=1, source_target_pairs={{8,0},{16,8},{24,16},{32,24},{40,32},{48,40},{56,48},{64,56},{72,6... | collective-permute-start | bytes 1572872 | tf_op jit(solution)/shard_map/ppermute | solution.py:12
  302.5 64.9 %copy-start.3 = (bf16[1024,1024]{1,0:T(8,128)(2,1)S(1)}, bf16[1024,1024]{1,0:T(8,128)(2,1)}, u32[]{:S(2)}) copy-start(bf16[1024,1024]{1,0:T(8,128)(2,1)} %all-gather.8.cloned.1.call-done) | copy-start | bytes 6291460
  363.6 60.4 %collective-permute-start.4 = (f32[1024,128]{0,1:T(8,128)}, f32[1024,128]{0,1:T(8,128)}, u32[]{:S(2)}, u32[]{:S(2)}) collective-permute-start(f32[1024,128]{0,1:T(8,128)} %convolution_add_fusion), channel_id=1, source_target_pairs={{8,0},{16,8},{24,16},{32,24},{40,32},{48,40},{56,48},{64,56},{72,6... | collective-permute-start | bytes 1572872 | tf_op jit(solution)/shard_map/ppermute | solution.py:12
  421.9 7.3 %copy-start = (bf16[1024,1024]{1,0:T(8,128)(2,1)S(1)}, bf16[1024,1024]{1,0:T(8,128)(2,1)}, u32[]{:S(2)}) copy-start(bf16[1024,1024]{1,0:T(8,128)(2,1)} %all-gather.10.cloned.1.call-done) | copy-start | bytes 6291460
  425.2 5.8 %copy-start.1 = (bf16[1024,1024]{1,0:T(8,128)(2,1)S(1)}, bf16[1024,1024]{1,0:T(8,128)(2,1)}, u32[]{:S(2)}) copy-start(bf16[1024,1024]{1,0:T(8,128)(2,1)} %all-gather.12.cloned.1.call-done) | copy-start | bytes 6291460
  425.2 11.5 %collective-permute-start.5 = (f32[1024,128]{0,1:T(8,128)S(1)}, f32[1024,128]{0,1:T(8,128)S(1)}, u32[]{:S(2)}, u32[]{:S(2)}) collective-permute-start(f32[1024,128]{0,1:T(8,128)S(1)} %add.45), channel_id=1, source_target_pairs={{8,0},{16,8},{24,16},{32,24},{40,32},{48,40},{56,48},{64,56},{72,6... | collective-permute-start | bytes 1572872 | tf_op jit(solution)/shard_map/ppermute | solution.py:12
  431.0 5.7 %copy-start.8 = (bf16[1024,1024]{1,0:T(8,128)(2,1)S(1)}, bf16[1024,1024]{1,0:T(8,128)(2,1)}, u32[]{:S(2)}) copy-start(bf16[1024,1024]{1,0:T(8,128)(2,1)} %all-gather.14.cloned.1.call-done) | copy-start | bytes 6291460
  431.0 5.7 %copy-start.9 = (f32[1024,128]{0,1:T(8,128)S(1)}, f32[1024,128]{0,1:T(8,128)}, u32[]{:S(2)}) copy-start(f32[1024,128]{0,1:T(8,128)} %fusion.20) | copy-start | bytes 1572868
Sparse Core Ops, SparseCore 0:
  25.5 63.1 all-gather.5
  175.8 62.5 all-gather.13
  240.5 59.1 all-gather.7
  301.6 59.1 all-gather.11
  362.7 59.1 all-gather.9
where the time goes:
time: 466 us; the launch traced here: 461 us
  waiting for transfers between devices  350 us (75%)
  blocking collectives  31.6 us (7%)
  starting transfers between devices  29.6 us (6%)
  matrix products  27.2 us (6%)
  between operations  13.4 us (3%)
  local copies, waits for them, and re-layouts  6.04 us (1%)
    all_gather x4, waiting for transfers between devices, per_device(): errors_all = lax.all_gather(errors, 'grp', axis=0, tiled=True)  221 us
    all_gather x1, waiting for transfers between devices, per_device(): visitor_full = lax.all_gather(unit_bf, 'grp', axis=1, tiled=True)  63.3 us
    ppermute x6, waiting for transfers between devices, passed_along(): return lax.ppermute(block, axis, route)  62.2 us
    ppermute x6, starting transfers between devices, passed_along(): return lax.ppermute(block, axis, route)  25 us
    psum x1, blocking collectives, per_device(): squares = lax.psum(jnp.sum(values * values, axis=1), 'grp')  16.8 us
    psum x1, blocking collectives, per_device(): inner = lax.psum(jnp.sum(unit * unit_grad, axis=1), 'grp')  14.8 us
    dot_general x4, matrix products, per_device(): lax.dot_general(errors_all, unit_bf, (((0,), (0,)), ((), ())), preferred_...  10.7 us
  transfers between devices with their start and end apart: 12, of which 10 were waited for; matrix products, arithmetic and copies ran while one was open for 6% of the time, Pallas kernels for 0%

commit v1 on v0

v1 whole, which is shorter than its diff:
```python
import functools

import jax
import jax.numpy as jnp
from jax import lax
from jax.experimental import pallas as pl
from jax.experimental.pallas import tpu as pltpu
from jax.sharding import PartitionSpec as P

MESH = pl.DeviceIdType.MESH
F32 = jnp.float32
BF16 = jnp.bfloat16
STEPS = 4


def to_lanes(column, eye):
    return jnp.sum(jnp.where(eye, column, 0.0), axis=0, keepdims=True)


def to_column(row, eye):
    return jnp.sum(jnp.where(eye, row, 0.0), axis=1, keepdims=True)


def kernel(
    n_loop, n_grp, s_ref, t_ref, out_ref,
    raw, unit, norm, rows_raw, rows_norm, urows, tiles, errors, own_send, own_recv, far_send, far_recv,
    own_total, own_rows, home_rows, inner_send, inner_recv,
    early_s, early_r, gather_s, gather_r, tile_s, tile_r, unit_s, unit_r, own_s, own_r, far_s, far_r,
    rows_s, rows_r, inner_s, inner_r,
):
    b = lax.axis_index("loop")
    g = lax.axis_index("grp")
    rows, width = s_ref.shape
    feats = width * n_grp
    part = rows // n_grp

    def mate(d):
        return lax.rem(g + 1 + d, n_grp)

    def below(k):
        return (lax.rem(b + n_loop - k, n_loop), g)

    def above(k):
        return (lax.rem(b + k, n_loop), g)

    def lanes(h, n=width):
        return pl.ds(pl.multiple_of(h * width, width), n)

    def part_of(h):
        return pl.ds(pl.multiple_of(h * part, part), part)

    def send(src, dst, s, r, to):
        copy = pltpu.make_async_remote_copy(
            src_ref=src, dst_ref=dst, send_sem=s, recv_sem=r, device_id=to, device_id_type=MESH
        )
        copy.start()
        return copy

    barrier = pltpu.get_barrier_semaphore()
    for d in range(n_grp - 1):
        pl.semaphore_signal(barrier, inc=1, device_id=(b, mate(d)), device_id_type=MESH)
    for k in range(1, STEPS):
        pl.semaphore_signal(barrier, inc=1, device_id=below(k), device_id_type=MESH)
        pl.semaphore_signal(barrier, inc=1, device_id=above(k), device_id_type=MESH)
    pl.semaphore_wait(barrier, n_grp - 1 + 2 * (STEPS - 1))

    early = [
        send(s_ref.at[part_of(mate(d)), :], rows_raw.at[:, lanes(g)], early_s.at[d], early_r.at[d], (b, mate(d)))
        for d in range(n_grp - 1)
    ]
    tile_copies = [
        send(t_ref.at[k], tiles.at[k - 1], tile_s.at[k - 1], tile_r.at[k - 1], below(k)) for k in range(1, STEPS)
    ]
    gather = [
        send(s_ref, raw.at[:, lanes(g)], gather_s.at[d], gather_r.at[d], (b, mate(d))) for d in range(n_grp - 1)
    ]
    raw[:, lanes(g)] = s_ref[...]
    rows_raw[:, lanes(g)] = s_ref[part_of(g), :]

    for copy in early:
        copy.wait_recv()
    values = rows_raw[...].astype(F32)
    row_norms = jnp.sqrt(jnp.sum(values * values, axis=1, keepdims=True) + 1e-06)
    rows_norm[...] = row_norms
    urows[0] = (values / row_norms).astype(BF16)
    unit_copies = [
        send(urows.at[0], urows.at[k], unit_s.at[k - 1], unit_r.at[k - 1], below(k)) for k in range(1, STEPS)
    ]

    for copy in gather:
        copy.wait_recv()

    def normalise(i, carry):
        at = pl.ds(pl.multiple_of(i * part, part), part)
        values = raw[at, :].astype(F32)
        norms = jnp.sqrt(jnp.sum(values * values, axis=1, keepdims=True) + 1e-06)
        norm[at, :] = norms
        unit[at, :] = (values / norms).astype(BF16)
        return carry

    lax.fori_loop(0, n_grp, normalise, 0)

    def error_tile(k, tile):
        mine = urows[k]

        def chunk(i, carry):
            at = pl.ds(pl.multiple_of(i * 256, 256), 256)
            similar = lax.dot_general(mine, unit[at, :], (((1,), (1,)), ((), ())), preferred_element_type=F32)
            errors[pl.ds(k * part, part), at] = (similar - tile[:, at].astype(F32)).astype(BF16)
            return carry

        lax.fori_loop(0, rows // 256, chunk, 0)

    def own_part(k, store):
        def chunk(i, carry):
            at = pl.ds(pl.multiple_of(i * 256, 256), 256)
            store(at, jnp.dot(errors[pl.ds(k * part, part), :], unit[:, at], preferred_element_type=F32))
            return carry

        lax.fori_loop(0, feats // 256, chunk, 0)

    def keep(at, value):
        own_total[:, at] = value

    error_tile(0, t_ref.at[0])
    own_part(0, keep)
    own_copies = []
    for k in range(1, STEPS):
        unit_copies[k - 1].wait_recv()
        tile_copies[k - 1].wait_recv()
        error_tile(k, tiles.at[k - 1])

        def put(at, value, k=k):
            own_send[k - 1, :, at] = value.astype(BF16)

        own_part(k, put)
        own_copies.append(
            send(own_send.at[k - 1], own_recv.at[k - 1], own_s.at[k - 1], own_r.at[k - 1], above(k))
        )

    far_copies = []
    for i in range(n_grp // 2):
        pair = lax.rem(lax.div(g, 2) + 1 + i, n_grp // 2)
        at = pl.ds(pl.multiple_of(pair * 2 * width, 2 * width), 2 * width)
        for j in range(STEPS):
            piece = lax.dot_general(
                errors[:, pl.ds(j * rows // STEPS, rows // STEPS)],
                urows[:, :, at].reshape(STEPS * part, 2 * width),
                (((0,), (0,)), ((), ())),
                preferred_element_type=F32,
            )
            far_send[pl.ds(j * rows // STEPS, rows // STEPS), at] = piece.astype(BF16)
        here = [pair * 2, pair * 2 + 1] if i < n_grp // 2 - 1 else [g + 1 - 2 * lax.rem(g, 2)]
        for h in here:
            n = len(far_copies)
            slot = lax.rem(g - h + n_grp + n_grp - 1, n_grp)
            far_copies.append(
                send(far_send.at[:, lanes(h)], far_recv.at[slot], far_s.at[n], far_r.at[slot], (b, h))
            )

    eye = lax.broadcasted_iota(jnp.int32, (part, part), 0) == lax.broadcasted_iota(jnp.int32, (part, part), 1)

    def inner_rows(i, carry):
        at = pl.ds(pl.multiple_of(i * part, part), part)
        dots = jnp.sum(raw[at, :].astype(F32) * far_send[at, :].astype(F32), axis=1, keepdims=True)
        inner_send[pl.ds(i, 1), :] = to_lanes(dots / norm[at, :], eye)
        return carry

    lax.fori_loop(0, n_grp, inner_rows, 0)

    for copy in own_copies:
        copy.wait_recv()
    total = own_total[...]
    for k in range(1, STEPS):
        total = total + own_recv[k - 1].astype(F32)
    rounded = total.astype(BF16)
    own_rows[...] = rounded
    rows_copies = [
        send(own_rows.at[:, lanes(mate(d))], home_rows.at[part_of(g), :], rows_s.at[d], rows_r.at[d], (b, mate(d)))
        for d in range(n_grp - 1)
    ]
    dots = jnp.sum(rows_raw[...].astype(F32) * rounded.astype(F32), axis=1, keepdims=True)
    inner_send[pl.ds(g, 1), :] = inner_send[pl.ds(g, 1), :] + to_lanes(dots / rows_norm[...], eye)
    inner_copies = [
        send(inner_send, inner_recv.at[d], inner_s.at[d], inner_r.at[d], (b, mate(d))) for d in range(n_grp - 1)
    ]
    home_rows[part_of(g), :] = own_rows[:, lanes(g)]

    for copy in rows_copies + inner_copies + far_copies:
        copy.wait_recv()

    inner = inner_send[...]
    for d in range(n_grp - 1):
        inner = inner + inner_recv[d]

    for i in range(n_grp):
        at = pl.ds(i * part, part)
        grad = home_rows[at, :].astype(F32) + far_send[at, lanes(g)].astype(F32)
        for d in range(n_grp - 1):
            grad = grad + far_recv[d, at, :].astype(F32)
        norms = norm[at, :]
        along = to_column(inner[i : i + 1, :], eye)
        out_ref[at, :] = 2.0 * (grad - (s_ref[at, :].astype(F32) / norms) * along) / norms

    for copy in early + tile_copies + gather + unit_copies + own_copies + far_copies + rows_copies + inner_copies:
        copy.wait_send()


def per_device(n_loop, n_grp, student, teacher_tiles):
    rows, width = student.shape
    feats = width * n_grp
    part = rows // n_grp
    mates, hops = n_grp - 1, STEPS - 1
    tiles = jnp.transpose(teacher_tiles, (1, 0, 2))
    dma = pltpu.SemaphoreType.DMA
    scratch = [
        pltpu.VMEM((rows, feats), BF16),
        pltpu.VMEM((rows, feats), BF16),
        pltpu.VMEM((rows, 1), F32),
        pltpu.VMEM((part, feats), BF16),
        pltpu.VMEM((part, 1), F32),
        pltpu.VMEM((STEPS, part, feats), BF16),
        pltpu.VMEM((hops, part, rows), BF16),
        pltpu.VMEM((STEPS * part, rows), BF16),
        pltpu.VMEM((hops, part, feats), BF16),
        pltpu.VMEM((hops, part, feats), BF16),
        pltpu.VMEM((rows, feats), BF16),
        pltpu.VMEM((mates, rows, width), BF16),
        pltpu.VMEM((part, feats), F32),
        pltpu.VMEM((part, feats), BF16),
        pltpu.VMEM((rows, width), BF16),
        pltpu.VMEM((n_grp, part), F32),
        pltpu.VMEM((mates, n_grp, part), F32),
    ]
    for count in (mates, mates, hops, hops, hops, mates, mates, mates):
        scratch += [dma((count,)), dma((count,))]
    return pl.pallas_call(
        functools.partial(kernel, n_loop, n_grp),
        out_shape=jax.ShapeDtypeStruct((rows, width), F32),
        in_specs=[pl.BlockSpec(memory_space=pltpu.VMEM)] * 2,
        out_specs=pl.BlockSpec(memory_space=pltpu.VMEM),
        scratch_shapes=scratch,
        compiler_params=pltpu.CompilerParams(
            collective_id=0, has_side_effects=True, vmem_limit_bytes=56 * 2**20
        ),
        name="window_grad",
    )(student, tiles)


def solution(mesh):
    placed = (P("loop", "grp"), P(("loop", "grp"), None, None))
    return jax.shard_map(
        functools.partial(per_device, mesh.shape["loop"], mesh.shape["grp"]),
        mesh=mesh, in_specs=placed, out_specs=P("loop", "grp"), check_vma=False,
    )
```

time: 466 us -> 117 us (0.25)
  the two profiles are of different devices: /device:TPU:1 before, /device:TPU:500 now
where the time goes in v1:
time: 117 us
  Pallas kernels  112 us (96%)
  local copies, waits for them, and re-layouts  4.4 us (4%)
    pallas_call x1, Pallas kernels, per_device(): pl.pallas_call(functools.partial(kernel, n_loop, n_grp), out_shape=jax.Sh...  112 us
    unnamed x2, local copies, waits for them, and re-layouts  4.4 us

profile of v1, /device:TPU:500, one launch (start us, length us, event | category | flops | bytes accessed | tf_op | source)
XLA Modules:
  0.0 116.6 jit_solution(15663886180764553235)
XLA Ops:
  0.0 2.5 %copy.5 = bf16[128,4,1024]{2,0,1:T(8,128)(2,1)} copy(bf16[128,4,1024]{2,1,0:T(4,128)(2,1)} %param.3) | data formatting | bytes 2097152 | tf_op args[1]
  2.5 112.2 %window_grad.1 = f32[1024,128]{1,0:T(8,128)} custom-call(bf16[1024,128]{1,0:T(8,128)(2,1)} %s_ref.1, bf16[4,128,1024]{2,1,0:T(8,128)(2,1)} %bitcast.3), custom_call_target="tpu_custom_call" | custom-call | tf_op jit(solution)/shard_map/window_grad/pallas_call | solution.py:237
  114.7 1.9 %copy.7 = f32[1024,128]{1,0:T(8,128)} copy(f32[1024,128]{1,0:T(8,128)} %window_grad.1) | data formatting | bytes 1048576

commit v2 on v1

v2 whole, which is shorter than its diff:
```python
import functools

import jax
import jax.numpy as jnp
from jax import lax
from jax.experimental import pallas as pl
from jax.experimental.pallas import tpu as pltpu
from jax.sharding import PartitionSpec as P

MESH = pl.DeviceIdType.MESH
F32 = jnp.float32
BF16 = jnp.bfloat16
STEPS = 4
HALVES = 2
G_SIDE, G_LEFT, G_LEFT_SIDE, G_RIGHT, G_RIGHT_SIDE, G_LEFT_FAR, G_RIGHT_FAR = range(7)
R_LEFT_PASS, R_RIGHT_PASS, R_LEFT, R_RIGHT, R_LEFT_SUM, R_RIGHT_SUM, R_SIDE = range(7)


def to_lanes(column, eye):
    return jnp.sum(jnp.where(eye, column, 0.0), axis=0, keepdims=True)


def to_column(row, eye):
    return jnp.sum(jnp.where(eye, row, 0.0), axis=1, keepdims=True)


def kernel(
    n_loop, n_grp, s_ref, t_ref, out_ref,
    raw, unit, squares, norm, rows_raw, rows_norm, urows, tiles, errors, own_send, own_recv,
    far, landed, passed, side, own_total, own_rows, home_rows, inner_send, inner_recv,
    early_s, early_r, gather_s, gather_r, tile_s, tile_r, unit_s, unit_r, own_s, own_r, far_s, far_r,
    rows_s, rows_r, inner_s, inner_r,
):
    b = lax.axis_index("loop")
    g = lax.axis_index("grp")
    rows, width = s_ref.shape
    feats = width * n_grp
    part = rows // n_grp
    half = rows // HALVES
    n_x = n_grp // 2
    x, y = lax.div(g, 2), lax.rem(g, 2)

    def at_x(dx, other=False):
        return lax.rem(x + dx + n_x, n_x) * 2 + (1 - y if other else y)

    def mate(d):
        return lax.rem(g + 1 + d, n_grp)

    def below(k):
        return (lax.rem(b + n_loop - k, n_loop), g)

    def above(k):
        return (lax.rem(b + k, n_loop), g)

    def part_of(h):
        return pl.ds(pl.multiple_of(h * part, part), part)

    started = []

    def send(src, dst, s, r, to):
        copy = pltpu.make_async_remote_copy(
            src_ref=src, dst_ref=dst, send_sem=s, recv_sem=r, device_id=to, device_id_type=MESH
        )
        copy.start()
        started.append(copy)
        return copy

    right, left, beside = (b, at_x(1)), (b, at_x(-1)), (b, at_x(0, True))

    barrier = pltpu.get_barrier_semaphore()
    for d in range(n_grp - 1):
        pl.semaphore_signal(barrier, inc=1, device_id=(b, mate(d)), device_id_type=MESH)
    for k in range(1, STEPS):
        pl.semaphore_signal(barrier, inc=1, device_id=below(k), device_id_type=MESH)
        pl.semaphore_signal(barrier, inc=1, device_id=above(k), device_id_type=MESH)
    pl.semaphore_wait(barrier, n_grp - 1 + 2 * (STEPS - 1))

    early = [
        send(s_ref.at[part_of(mate(d)), :], rows_raw.at[g], early_s.at[d], early_r.at[d], (b, mate(d)))
        for d in range(n_grp - 1)
    ]
    sent_slices = []

    def give(src, h, slot, to):
        n = len(sent_slices)
        sent_slices.append(send(src, raw.at[h], gather_s.at[n], gather_r.at[slot], to))

    def take(slot):
        pltpu.make_async_copy(raw.at[0], raw.at[0], gather_r.at[slot]).wait()

    give(s_ref, g, G_SIDE, beside)
    give(s_ref, g, G_LEFT, right)
    give(s_ref, g, G_RIGHT, left)

    def send_tile(k):
        return send(t_ref.at[k], tiles.at[k - 1], tile_s.at[k - 1], tile_r.at[k - 1], below(k))

    def send_unit(k):
        return send(urows.at[k], urows.at[k + 1], unit_s.at[k], unit_r.at[k], below(1))

    tile_copies = {3: send_tile(3)}
    raw[g] = s_ref[...]
    rows_raw[g] = s_ref[part_of(g), :]

    def add_squares(h, first=False):
        def block(i, carry):
            at = pl.ds(pl.multiple_of(i * part, part), part)
            values = raw[h, at, :].astype(F32)
            squares[at, :] = values * values if first else squares[at, :] + values * values
            return carry

        lax.fori_loop(0, n_grp, block, 0)

    for copy in early:
        copy.wait_recv()
    total = jnp.zeros((part, width), F32)
    for h in range(n_grp):
        values = rows_raw[h].astype(F32)
        total = total + values * values
    norms = jnp.sqrt(jnp.sum(total, axis=1, keepdims=True) + 1e-06)
    rows_norm[...] = norms
    for h in range(n_grp):
        urows[0, :, h * width : (h + 1) * width] = (rows_raw[h].astype(F32) / norms).astype(BF16)
    unit_copies = [send_unit(0)]
    tile_copies[2] = send_tile(2)
    add_squares(g, first=True)

    take(G_SIDE)
    give(raw.at[at_x(0, True)], at_x(0, True), G_LEFT_SIDE, right)
    take(G_LEFT)
    give(raw.at[at_x(-1)], at_x(-1), G_LEFT_FAR, right)
    give(raw.at[at_x(0, True)], at_x(0, True), G_RIGHT_SIDE, left)
    add_squares(at_x(0, True))
    add_squares(at_x(-1))
    unit_copies[0].wait_recv()
    unit_copies.append(send_unit(1))
    tile_copies[1] = send_tile(1)
    take(G_RIGHT)
    add_squares(at_x(1))
    take(G_RIGHT_SIDE)
    give(raw.at[at_x(1, True)], at_x(1, True), G_RIGHT_FAR, left)
    add_squares(at_x(1, True))
    unit_copies[1].wait_recv()
    unit_copies.append(send_unit(2))
    take(G_LEFT_SIDE)
    add_squares(at_x(-1, True))
    take(G_LEFT_FAR)
    add_squares(at_x(-2))
    take(G_RIGHT_FAR)
    add_squares(at_x(2, True))

    def normalise(i, carry):
        at = pl.ds(pl.multiple_of(i * part, part), part)
        norms = jnp.sqrt(jnp.sum(squares[at, :], axis=1, keepdims=True) + 1e-06)
        norm[at, :] = norms
        inverse = 1.0 / norms
        for h in range(n_grp):
            unit[at, h * width : (h + 1) * width] = (raw[h, at, :].astype(F32) * inverse).astype(BF16)
        return carry

    lax.fori_loop(0, n_grp, normalise, 0)

    def error_tile(k, tile):
        mine = urows[k]

        def chunk(i, carry):
            at = pl.ds(pl.multiple_of(i * 256, 256), 256)
            similar = lax.dot_general(mine, unit[at, :], (((1,), (1,)), ((), ())), preferred_element_type=F32)
            errors[pl.ds(k * part, part), at] = (similar - tile[:, at].astype(F32)).astype(BF16)
            return carry

        lax.fori_loop(0, rows // 256, chunk, 0)

    def own_part(k, store):
        def chunk(i, carry):
            at = pl.ds(pl.multiple_of(i * 256, 256), 256)
            store(at, jnp.dot(errors[pl.ds(k * part, part), :], unit[:, at], preferred_element_type=F32))
            return carry

        lax.fori_loop(0, feats // 256, chunk, 0)

    def keep(at, value):
        own_total[:, at] = value

    error_tile(0, t_ref.at[0])
    own_part(0, keep)
    own_copies = []
    for k in range(1, STEPS):
        if k == STEPS - 1:
            unit_copies[k - 1].wait_recv()
        tile_copies[k].wait_recv()
        error_tile(k, tiles.at[k - 1])

        def put(at, value, k=k):
            own_send[k - 1, :, at] = value.astype(BF16)

        own_part(k, put)
        own_copies.append(
            send(own_send.at[k - 1], own_recv.at[k - 1], own_s.at[k - 1], own_r.at[k - 1], above(k))
        )

    def far_pair(dx):
        pair = lax.rem(x + dx + n_x, n_x)
        mine = urows[:, :, pl.ds(pl.multiple_of(pair * 2 * width, 2 * width), 2 * width)].reshape(
            STEPS * part, 2 * width
        )

        def chunk(i, carry):
            at = pl.ds(pl.multiple_of(i * 256, 256), 256)
            piece = lax.dot_general(
                errors[:, at], mine, (((0,), (0,)), ((), ())), preferred_element_type=F32
            ).astype(BF16)
            far[pair * 2, at, :] = piece[:, :width]
            far[pair * 2 + 1, at, :] = piece[:, width:]
            return carry

        lax.fori_loop(0, rows // 256, chunk, 0)

    sent_sums = []

    def hand(src, slot, to, i=None):
        n = len(sent_sums)
        dst, r = landed.at[slot], far_r.at[slot, 0]
        if i is not None:
            src, dst, r = src.at[pl.ds(i * half, half), :], dst.at[pl.ds(i * half, half), :], far_r.at[slot, i]
        sent_sums.append(send(src, dst, far_s.at[n], r, to))

    def got(slot, i=None):
        at = pl.ds(0, rows) if i is None else pl.ds(i * half, half)
        here = landed.at[slot, at, :]
        pltpu.make_async_copy(here, here, far_r.at[slot, i or 0]).wait()

    far_pair(2)
    hand(far.at[at_x(2, True)], R_LEFT_PASS, right)
    hand(far.at[at_x(2)], R_RIGHT_PASS, left)
    far_pair(1)
    hand(far.at[at_x(1)], R_LEFT, right)
    far_pair(-1)
    hand(far.at[at_x(-1, True)], R_RIGHT, left)
    far_pair(0)

    eye = lax.broadcasted_iota(jnp.int32, (part, part), 0) == lax.broadcasted_iota(jnp.int32, (part, part), 1)

    def inner_rows(i, carry):
        at = pl.ds(pl.multiple_of(i * part, part), part)
        dots = jnp.zeros((part, width), F32)
        for h in range(n_grp):
            dots = dots + raw[h, at, :].astype(F32) * far[h, at, :].astype(F32)
        inner_send[pl.ds(i, 1), :] = to_lanes(jnp.sum(dots, axis=1, keepdims=True) / norm[at, :], eye)
        return carry

    lax.fori_loop(0, n_grp, inner_rows, 0)

    got(R_LEFT_PASS)
    got(R_RIGHT_PASS)
    for i in range(HALVES):
        at = pl.ds(i * half, half)
        passed[0, at, :] = (far[at_x(1, True), at, :].astype(F32) + landed[R_LEFT_PASS, at, :].astype(F32)).astype(BF16)
        hand(passed.at[0], R_LEFT_SUM, right, i)
        passed[1, at, :] = (far[at_x(-1), at, :].astype(F32) + landed[R_RIGHT_PASS, at, :].astype(F32)).astype(BF16)
        hand(passed.at[1], R_RIGHT_SUM, left, i)

    for copy in own_copies:
        copy.wait_recv()
    total = own_total[...]
    for k in range(1, STEPS):
        total = total + own_recv[k - 1].astype(F32)
    dots = jnp.zeros((part, width), F32)
    for h in range(n_grp):
        rounded = total[:, h * width : (h + 1) * width].astype(BF16)
        own_rows[h] = rounded
        dots = dots + rows_raw[h].astype(F32) * rounded.astype(F32)
    rows_copies = [
        send(own_rows.at[mate(d)], home_rows.at[part_of(g), :], rows_s.at[d], rows_r.at[d], (b, mate(d)))
        for d in range(n_grp - 1)
    ]
    inner_send[pl.ds(g, 1), :] = inner_send[pl.ds(g, 1), :] + to_lanes(
        jnp.sum(dots, axis=1, keepdims=True) / rows_norm[...], eye
    )
    inner_copies = [
        send(inner_send, inner_recv.at[d], inner_s.at[d], inner_r.at[d], (b, mate(d))) for d in range(n_grp - 1)
    ]
    home_rows[part_of(g), :] = own_rows[g]

    got(R_LEFT)
    got(R_RIGHT)
    for i in range(HALVES):
        at = pl.ds(i * half, half)
        got(R_LEFT_SUM, i)
        side[at, :] = (
            far[at_x(0, True), at, :].astype(F32)
            + landed[R_RIGHT, at, :].astype(F32)
            + landed[R_LEFT_SUM, at, :].astype(F32)
        ).astype(BF16)
        hand(side, R_SIDE, beside, i)

    for copy in rows_copies + inner_copies:
        copy.wait_recv()
    inner = inner_send[...]
    for d in range(n_grp - 1):
        inner = inner + inner_recv[d]

    for i in range(n_grp):
        if i % (n_grp // HALVES) == 0:
            got(R_RIGHT_SUM, i // (n_grp // HALVES))
            got(R_SIDE, i // (n_grp // HALVES))
        at = pl.ds(i * part, part)
        grad = home_rows[at, :].astype(F32) + far[g, at, :].astype(F32)
        for slot in (R_LEFT, R_RIGHT_SUM, R_SIDE):
            grad = grad + landed[slot, at, :].astype(F32)
        norms = norm[at, :]
        along = to_column(inner[i : i + 1, :], eye)
        out_ref[at, :] = 2.0 * (grad - (s_ref[at, :].astype(F32) / norms) * along) / norms

    for copy in started:
        copy.wait_send()


def per_device(n_loop, n_grp, student, teacher_tiles):
    rows, width = student.shape
    feats = width * n_grp
    part = rows // n_grp
    mates, hops = n_grp - 1, STEPS - 1
    tiles = jnp.transpose(teacher_tiles, (1, 0, 2))
    dma = pltpu.SemaphoreType.DMA
    scratch = [
        pltpu.VMEM((n_grp, rows, width), BF16),
        pltpu.VMEM((rows, feats), BF16),
        pltpu.VMEM((rows, width), F32),
        pltpu.VMEM((rows, 1), F32),
        pltpu.VMEM((n_grp, part, width), BF16),
        pltpu.VMEM((part, 1), F32),
        pltpu.VMEM((STEPS, part, feats), BF16),
        pltpu.VMEM((hops, part, rows), BF16),
        pltpu.VMEM((STEPS * part, rows), BF16),
        pltpu.VMEM((hops, part, feats), BF16),
        pltpu.VMEM((hops, part, feats), BF16),
        pltpu.VMEM((n_grp, rows, width), BF16),
        pltpu.VMEM((7, rows, width), BF16),
        pltpu.VMEM((2, rows, width), BF16),
        pltpu.VMEM((rows, width), BF16),
        pltpu.VMEM((part, feats), F32),
        pltpu.VMEM((n_grp, part, width), BF16),
        pltpu.VMEM((rows, width), BF16),
        pltpu.VMEM((n_grp, part), F32),
        pltpu.VMEM((mates, n_grp, part), F32),
        dma((mates,)), dma((mates,)),
        dma((7,)), dma((7,)),
        dma((hops,)), dma((hops,)),
        dma((hops,)), dma((hops,)),
        dma((hops,)), dma((hops,)),
        dma((4 + 3 * HALVES,)), dma((7, HALVES)),
        dma((mates,)), dma((mates,)),
        dma((mates,)), dma((mates,)),
    ]
    return pl.pallas_call(
        functools.partial(kernel, n_loop, n_grp),
        out_shape=jax.ShapeDtypeStruct((rows, width), F32),
        in_specs=[pl.BlockSpec(memory_space=pltpu.VMEM)] * 2,
        out_specs=pl.BlockSpec(memory_space=pltpu.VMEM),
        scratch_shapes=scratch,
        compiler_params=pltpu.CompilerParams(
            collective_id=0, has_side_effects=True, vmem_limit_bytes=56 * 2**20
        ),
        name="window_grad",
    )(student, tiles)


def solution(mesh):
    placed = (P("loop", "grp"), P(("loop", "grp"), None, None))
    return jax.shard_map(
        functools.partial(per_device, mesh.shape["loop"], mesh.shape["grp"]),
        mesh=mesh, in_specs=placed, out_specs=P("loop", "grp"), check_vma=False,
    )
```

time: 117 us -> 98.8 us (0.84)
  the two profiles are of different devices: /device:TPU:500 before, /device:TPU:1 now
where the time goes in v2:
time: 98.8 us; the launch traced here: 98.6 us
  Pallas kernels  94.2 us (95%)
  local copies, waits for them, and re-layouts  4.4 us (4%)
    pallas_call x1, Pallas kernels, per_device(): pl.pallas_call(functools.partial(kernel, n_loop, n_grp), out_shape=jax.Sh...  94.2 us
    unnamed x2, local copies, waits for them, and re-layouts  4.4 us

profile of v2, /device:TPU:1, one launch (start us, length us, event | category | flops | bytes accessed | tf_op | source)
XLA Modules:
  0.0 98.6 jit_solution(17171555414536813359)
XLA Ops:
  0.0 2.5 %copy.5 = bf16[128,4,1024]{2,0,1:T(8,128)(2,1)} copy(bf16[128,4,1024]{2,1,0:T(4,128)(2,1)} %param.3) | data formatting | bytes 2097152 | tf_op args[1]
  2.5 94.2 %window_grad.1 = f32[1024,128]{1,0:T(8,128)} custom-call(bf16[1024,128]{1,0:T(8,128)(2,1)} %s_ref.1, bf16[4,128,1024]{2,1,0:T(8,128)(2,1)} %bitcast.3), custom_call_target="tpu_custom_call" | custom-call | tf_op jit(solution)/shard_map/window_grad/pallas_call | solution.py:356
  96.7 1.9 %copy.7 = f32[1024,128]{1,0:T(8,128)} copy(f32[1024,128]{1,0:T(8,128)} %window_grad.1) | data formatting | bytes 1048576

commit v3 on v2

v3 whole, which is shorter than its diff:
```python
import functools

import jax
import jax.numpy as jnp
from jax import lax
from jax.experimental import pallas as pl
from jax.experimental.pallas import tpu as pltpu
from jax.sharding import PartitionSpec as P

MESH = pl.DeviceIdType.MESH
F32 = jnp.float32
BF16 = jnp.bfloat16
STEPS = 4
HALVES = 2
G_SIDE, G_LEFT, G_LEFT_SIDE, G_RIGHT, G_RIGHT_SIDE, G_LEFT_FAR, G_RIGHT_FAR = range(7)
R_LEFT_PASS, R_RIGHT_PASS, R_LEFT, R_RIGHT, R_LEFT_SUM, R_RIGHT_SUM, R_SIDE = range(7)


def to_lanes(column, eye):
    return jnp.sum(jnp.where(eye, column, 0.0), axis=0, keepdims=True)


def to_column(row, eye):
    return jnp.sum(jnp.where(eye, row, 0.0), axis=1, keepdims=True)


def kernel(
    n_loop, n_grp, s_ref, t_ref, out_ref,
    raw, unit, squares, norm, rows_raw, rows_norm, urows, sent_tiles, tiles, third, errors, errors_t, own_send, own_recv,
    far, landed, passed, side, own_total, own_rows, home_rows, inner_send, inner_recv,
    early_s, early_r, gather_s, gather_r, tile_s, tile_r, third_s, third_r, unit_s, unit_r, own_s, own_r, far_s, far_r,
    rows_s, rows_r, inner_s, inner_r,
):
    b = lax.axis_index("loop")
    g = lax.axis_index("grp")
    rows, width = s_ref.shape
    feats = width * n_grp
    part = rows // n_grp
    half = rows // HALVES
    step = min(256, half)
    n_x = n_grp // 2
    x, y = lax.div(g, 2), lax.rem(g, 2)

    def at_x(dx, other=False):
        return lax.rem(x + dx + n_x, n_x) * 2 + (1 - y if other else y)

    def mate(d):
        return lax.rem(g + 1 + d, n_grp)

    def block(k):
        return (lax.rem(b + n_loop + k, n_loop), g)

    def part_of(h):
        return pl.ds(pl.multiple_of(h * part, part), part)

    def half_of(i):
        return pl.ds(i * half, half)

    started = []

    def send(src, dst, s, r, to):
        copy = pltpu.make_async_remote_copy(
            src_ref=src, dst_ref=dst, send_sem=s, recv_sem=r, device_id=to, device_id_type=MESH
        )
        copy.start()
        started.append(copy)
        return copy

    right, left, beside = (b, at_x(1)), (b, at_x(-1)), (b, at_x(0, True))

    barrier = pltpu.get_barrier_semaphore()
    for d in range(n_grp - 1):
        pl.semaphore_signal(barrier, inc=1, device_id=(b, mate(d)), device_id_type=MESH)
    for k in range(1, STEPS):
        pl.semaphore_signal(barrier, inc=1, device_id=block(-k), device_id_type=MESH)
        pl.semaphore_signal(barrier, inc=1, device_id=block(k), device_id_type=MESH)

    tiles[pl.ds(0, part), :] = t_ref[:, 0, :]
    for k in range(1, STEPS - 1):
        sent_tiles[k - 1] = t_ref[:, k, :]
    last = t_ref[:, STEPS - 1, :]
    for h in range(n_grp):
        third[0, h] = last[:, h * part : (h + 1) * part]
    raw[g] = s_ref[...]
    rows_raw[g] = s_ref[part_of(g), :]

    def add_squares(h, i, first=False):
        def piece(j, carry):
            at = pl.ds(pl.multiple_of(i * half + j * part, part), part)
            values = raw[h, at, :].astype(F32)
            squares[at, :] = values * values if first else squares[at, :] + values * values
            return carry

        lax.fori_loop(0, half // part, piece, 0)

    for i in range(HALVES):
        add_squares(g, i, first=True)

    pl.semaphore_wait(barrier, n_grp - 1 + 2 * (STEPS - 1))

    early = [
        send(s_ref.at[part_of(mate(d)), :], rows_raw.at[g], early_s.at[d], early_r.at[d], (b, mate(d)))
        for d in range(n_grp - 1)
    ]
    sent_slices = []

    def give(h, i, slot, to, src=None):
        n = len(sent_slices)
        src = raw.at[h] if src is None else src
        sent_slices.append(
            send(src.at[half_of(i), :], raw.at[h, half_of(i), :], gather_s.at[n], gather_r.at[slot, i], to)
        )

    def take(slot, h, i):
        here = raw.at[h, half_of(i), :]
        pltpu.make_async_copy(here, here, gather_r.at[slot, i]).wait()

    for i in range(HALVES):
        give(g, i, G_SIDE, beside, s_ref)
        give(g, i, G_LEFT, right, s_ref)
        give(g, i, G_RIGHT, left, s_ref)

    def send_tile(k):
        dst = tiles.at[pl.ds(k * part, part), :]
        return send(sent_tiles.at[k - 1], dst, tile_s.at[k - 1], tile_r.at[k - 1], block(-k))

    def urow(k):
        return urows.at[pl.ds(k * part, part), :]

    tile_copies = [send_tile(2), send_tile(1)]
    third_copies = [
        send(third.at[0, mate(d)], third.at[1, g], third_s.at[d], third_r.at[d], (b, mate(d)))
        for d in range(n_grp - 1)
    ]
    third[1, g] = third[0, g]

    for copy in early:
        copy.wait_recv()
    total = jnp.zeros((part, width), F32)
    for h in range(n_grp):
        values = rows_raw[h].astype(F32)
        total = total + values * values
    norms = jnp.sqrt(jnp.sum(total, axis=1, keepdims=True) + 1e-06)
    rows_norm[...] = norms
    for h in range(n_grp):
        urows[0:part, h * width : (h + 1) * width] = (rows_raw[h].astype(F32) / norms).astype(BF16)
    unit_copies = [
        send(urow(0), urow(1), unit_s.at[0], unit_r.at[0], block(-1)),
        send(urow(0), urow(3), unit_s.at[2], unit_r.at[2], block(3)),
    ]

    def pass_on(i):
        take(G_SIDE, at_x(0, True), i)
        give(at_x(0, True), i, G_LEFT_SIDE, right)
        give(at_x(0, True), i, G_RIGHT_SIDE, left)
        take(G_LEFT, at_x(-1), i)
        give(at_x(-1), i, G_LEFT_FAR, right)

    def pass_back(i):
        take(G_RIGHT_SIDE, at_x(1, True), i)
        give(at_x(1, True), i, G_RIGHT_FAR, left)

    def use(i, *slices):
        for h in slices:
            add_squares(h, i)

    pass_on(0)
    use(0, at_x(0, True), at_x(-1))
    unit_copies[0].wait_recv()
    unit_copies.append(send(urow(1), urow(2), unit_s.at[1], unit_r.at[1], block(-1)))
    pass_on(1)
    pass_back(0)
    use(0, at_x(1, True))
    take(G_RIGHT, at_x(1), 0)
    take(G_LEFT_SIDE, at_x(-1, True), 0)
    use(0, at_x(1), at_x(-1, True))
    take(G_LEFT_FAR, at_x(-2), 0)
    use(0, at_x(-2))
    use(1, at_x(0, True), at_x(-1))
    for copy in third_copies:
        copy.wait_recv()
    for h in range(n_grp):
        tiles[3 * part : 4 * part, h * part : (h + 1) * part] = third[1, h].astype(F32).T.astype(BF16)
    take(G_RIGHT_FAR, at_x(2, True), 0)
    use(0, at_x(2, True))
    pass_back(1)

    def normalise(i):
        def piece(j, carry):
            at = pl.ds(pl.multiple_of(i * half + j * part, part), part)
            norms = jnp.sqrt(jnp.sum(squares[at, :], axis=1, keepdims=True) + 1e-06)
            norm[at, :] = norms
            inverse = 1.0 / norms
            for h in range(n_grp):
                unit[at, h * width : (h + 1) * width] = (raw[h, at, :].astype(F32) * inverse).astype(BF16)
            return carry

        lax.fori_loop(0, half // part, piece, 0)

    def error_tiles(i):
        def piece(j, carry):
            at = pl.ds(pl.multiple_of(i * half + j * step, step), step)
            similar = lax.dot_general(
                urows[...], unit[at, :], (((1,), (1,)), ((), ())), preferred_element_type=F32
            )
            found = similar - tiles[:, at].astype(F32)
            errors[:, at] = found.astype(BF16)
            errors_t[at, :] = found.T.astype(BF16)
            return carry

        lax.fori_loop(0, half // step, piece, 0)

    def far_pair(dx, i):
        pair = lax.rem(x + dx + n_x, n_x)
        mine = urows[:, pl.ds(pl.multiple_of(pair * 2 * width, 2 * width), 2 * width)]

        def piece(j, carry):
            at = pl.ds(pl.multiple_of(i * half + j * step, step), step)
            sums = jnp.dot(errors_t[at, :], mine, preferred_element_type=F32).astype(BF16)
            far[pair * 2, at, :] = sums[:, :width]
            far[pair * 2 + 1, at, :] = sums[:, width:]
            return carry

        lax.fori_loop(0, half // step, piece, 0)

    sent_sums = []

    def hand(src, i, slot, to):
        n = len(sent_sums)
        sent_sums.append(
            send(src.at[half_of(i), :], landed.at[slot, half_of(i), :], far_s.at[n], far_r.at[slot, i], to)
        )

    def got(slot, i):
        here = landed.at[slot, half_of(i), :]
        pltpu.make_async_copy(here, here, far_r.at[slot, i]).wait()

    def far_terms(i):
        far_pair(2, i)
        hand(far.at[at_x(2, True)], i, R_LEFT_PASS, right)
        hand(far.at[at_x(2)], i, R_RIGHT_PASS, left)
        far_pair(1, i)
        hand(far.at[at_x(1)], i, R_LEFT, right)
        far_pair(-1, i)
        hand(far.at[at_x(-1, True)], i, R_RIGHT, left)
        far_pair(0, i)

    def add_passed(i):
        at = half_of(i)
        got(R_LEFT_PASS, i)
        passed[0, at, :] = (far[at_x(1, True), at, :].astype(F32) + landed[R_LEFT_PASS, at, :].astype(F32)).astype(BF16)
        hand(passed.at[0], i, R_LEFT_SUM, right)
        got(R_RIGHT_PASS, i)
        passed[1, at, :] = (far[at_x(-1), at, :].astype(F32) + landed[R_RIGHT_PASS, at, :].astype(F32)).astype(BF16)
        hand(passed.at[1], i, R_RIGHT_SUM, left)

    def add_side(i):
        at = half_of(i)
        got(R_RIGHT, i)
        got(R_LEFT_SUM, i)
        side[at, :] = (
            far[at_x(0, True), at, :].astype(F32)
            + landed[R_RIGHT, at, :].astype(F32)
            + landed[R_LEFT_SUM, at, :].astype(F32)
        ).astype(BF16)
        hand(side, i, R_SIDE, beside)

    for copy in tile_copies + unit_copies[1:]:
        copy.wait_recv()
    normalise(0)
    error_tiles(0)
    far_terms(0)

    use(1, at_x(1, True))
    take(G_RIGHT, at_x(1), 1)
    take(G_LEFT_SIDE, at_x(-1, True), 1)
    use(1, at_x(1), at_x(-1, True))
    take(G_LEFT_FAR, at_x(-2), 1)
    take(G_RIGHT_FAR, at_x(2, True), 1)
    use(1, at_x(-2), at_x(2, True))
    normalise(1)
    error_tiles(1)

    def own_parts(j, carry):
        at = pl.ds(pl.multiple_of(j * 256, 256), 256)
        found = jnp.dot(errors[...], unit[:, at], preferred_element_type=F32)
        own_total[:, at] = found[:part]
        for k in range(1, STEPS):
            own_send[k - 1, :, at] = found[k * part : (k + 1) * part].astype(BF16)
        return carry

    lax.fori_loop(0, feats // 256, own_parts, 0)
    own_copies = [
        send(own_send.at[k - 1], own_recv.at[k - 1], own_s.at[k - 1], own_r.at[k - 1], block(k if k < 3 else -3))
        for k in range(1, STEPS)
    ]
    far_terms(1)
    add_passed(0)

    eye = lax.broadcasted_iota(jnp.int32, (part, part), 0) == lax.broadcasted_iota(jnp.int32, (part, part), 1)

    def inner_rows(i, carry):
        at = pl.ds(pl.multiple_of(i * part, part), part)
        dots = jnp.zeros((part, width), F32)
        for h in range(n_grp):
            dots = dots + raw[h, at, :].astype(F32) * far[h, at, :].astype(F32)
        inner_send[pl.ds(i, 1), :] = to_lanes(jnp.sum(dots, axis=1, keepdims=True) / norm[at, :], eye)
        return carry

    lax.fori_loop(0, n_grp, inner_rows, 0)
    add_passed(1)

    for copy in own_copies:
        copy.wait_recv()
    total = own_total[...]
    for k in range(1, STEPS):
        total = total + own_recv[k - 1].astype(F32)
    dots = jnp.zeros((part, width), F32)
    for h in range(n_grp):
        rounded = total[:, h * width : (h + 1) * width].astype(BF16)
        own_rows[h] = rounded
        dots = dots + rows_raw[h].astype(F32) * rounded.astype(F32)
    rows_copies = [
        send(own_rows.at[mate(d)], home_rows.at[part_of(g), :], rows_s.at[d], rows_r.at[d], (b, mate(d)))
        for d in range(n_grp - 1)
    ]
    inner_send[pl.ds(g, 1), :] = inner_send[pl.ds(g, 1), :] + to_lanes(
        jnp.sum(dots, axis=1, keepdims=True) / rows_norm[...], eye
    )
    inner_copies = [
        send(inner_send, inner_recv.at[d], inner_s.at[d], inner_r.at[d], (b, mate(d))) for d in range(n_grp - 1)
    ]
    home_rows[part_of(g), :] = own_rows[g]

    for i in range(HALVES):
        add_side(i)

    for copy in rows_copies + inner_copies:
        copy.wait_recv()
    inner = inner_send[...]
    for d in range(n_grp - 1):
        inner = inner + inner_recv[d]

    for i in range(n_grp):
        if i % (n_grp // HALVES) == 0:
            for slot in (R_LEFT, R_RIGHT_SUM, R_SIDE):
                got(slot, i // (n_grp // HALVES))
        at = pl.ds(i * part, part)
        grad = home_rows[at, :].astype(F32) + far[g, at, :].astype(F32)
        for slot in (R_LEFT, R_RIGHT_SUM, R_SIDE):
            grad = grad + landed[slot, at, :].astype(F32)
        inverse = 1.0 / norm[at, :]
        along = to_column(inner[i : i + 1, :], eye)
        out_ref[at, :] = (2.0 * inverse) * (grad - s_ref[at, :].astype(F32) * (inverse * along))

    for copy in started:
        copy.wait_send()


def per_device(n_loop, n_grp, student, teacher_tiles):
    rows, width = student.shape
    feats = width * n_grp
    part = rows // n_grp
    mates, hops = n_grp - 1, STEPS - 1
    dma = pltpu.SemaphoreType.DMA
    scratch = [
        pltpu.VMEM((n_grp, rows, width), BF16),
        pltpu.VMEM((rows, feats), BF16),
        pltpu.VMEM((rows, width), F32),
        pltpu.VMEM((rows, 1), F32),
        pltpu.VMEM((n_grp, part, width), BF16),
        pltpu.VMEM((part, 1), F32),
        pltpu.VMEM((STEPS * part, feats), BF16),
        pltpu.VMEM((hops - 1, part, rows), BF16),
        pltpu.VMEM((STEPS * part, rows), BF16),
        pltpu.VMEM((2, n_grp, part, part), BF16),
        pltpu.VMEM((STEPS * part, rows), BF16),
        pltpu.VMEM((rows, STEPS * part), BF16),
        pltpu.VMEM((hops, part, feats), BF16),
        pltpu.VMEM((hops, part, feats), BF16),
        pltpu.VMEM((n_grp, rows, width), BF16),
        pltpu.VMEM((7, rows, width), BF16),
        pltpu.VMEM((2, rows, width), BF16),
        pltpu.VMEM((rows, width), BF16),
        pltpu.VMEM((part, feats), F32),
        pltpu.VMEM((n_grp, part, width), BF16),
        pltpu.VMEM((rows, width), BF16),
        pltpu.VMEM((n_grp, part), F32),
        pltpu.VMEM((mates, n_grp, part), F32),
        dma((mates,)), dma((mates,)),
        dma((7 * HALVES,)), dma((7, HALVES)),
        dma((hops - 1,)), dma((hops - 1,)),
        dma((mates,)), dma((mates,)),
        dma((hops,)), dma((hops,)),
        dma((hops,)), dma((hops,)),
        dma((7 * HALVES,)), dma((7, HALVES)),
        dma((mates,)), dma((mates,)),
        dma((mates,)), dma((mates,)),
    ]
    return pl.pallas_call(
        functools.partial(kernel, n_loop, n_grp),
        out_shape=jax.ShapeDtypeStruct((rows, width), F32),
        in_specs=[pl.BlockSpec(memory_space=pltpu.VMEM)] * 2,
        out_specs=pl.BlockSpec(memory_space=pltpu.VMEM),
        scratch_shapes=scratch,
        compiler_params=pltpu.CompilerParams(
            collective_id=0, has_side_effects=True, vmem_limit_bytes=56 * 2**20
        ),
        name="window_grad",
    )(student, teacher_tiles)


def solution(mesh):
    placed = (P("loop", "grp"), P(("loop", "grp"), None, None))
    return jax.shard_map(
        functools.partial(per_device, mesh.shape["loop"], mesh.shape["grp"]),
        mesh=mesh, in_specs=placed, out_specs=P("loop", "grp"), check_vma=False,
    )
```

time: 98.8 us -> 81.2 us (0.82)
  Pallas kernels: 94.2 us -> 78.6 us
  local copies, waits for them, and re-layouts: 4.4 us -> 1.87 us
    pallas_call x1, Pallas kernels: 94.2 us -> 78.6 us  [per_device(): pl.pallas_call(functools.partial(kernel, n_loop, n_grp), out_shape=jax.Sh...]
    unnamed x2 -> x1, local copies, waits for them, and re-layouts: 4.4 us -> 1.87 us
where the time goes in v3:
time: 81.2 us; the launch traced here: 80.5 us
  Pallas kernels  78.6 us (97%)
  local copies, waits for them, and re-layouts  1.87 us (2%)
    pallas_call x1, Pallas kernels, per_device(): pl.pallas_call(functools.partial(kernel, n_loop, n_grp), out_shape=jax.Sh...  78.6 us
    unnamed x1, local copies, waits for them, and re-layouts  1.87 us

profile of v3, /device:TPU:1, one launch (start us, length us, event | category | flops | bytes accessed | tf_op | source)
XLA Modules:
  0.0 80.5 jit_solution(835515745812650144)
XLA Ops:
  0.0 78.6 %window_grad.1 = f32[1024,128]{1,0:T(8,128)} custom-call(bf16[1024,128]{1,0:T(8,128)(2,1)} %s_ref.1, bf16[128,4,1024]{2,1,0:T(4,128)(2,1)} %t_ref.1), custom_call_target="tpu_custom_call" | custom-call | tf_op jit(solution)/shard_map/window_grad/pallas_call | solution.py:400
  78.6 1.9 %copy.4 = f32[1024,128]{1,0:T(8,128)} copy(f32[1024,128]{1,0:T(8,128)} %window_grad.1) | data formatting | bytes 1048576

commit v4 on v3

--- a/solution.py
+++ b/solution.py
@@ -28,7 +28,7 @@
     n_loop, n_grp, s_ref, t_ref, out_ref,
     raw, unit, squares, norm, rows_raw, rows_norm, urows, sent_tiles, tiles, third, errors, errors_t, own_send, own_recv,
     far, landed, passed, side, own_total, own_rows, home_rows, inner_send, inner_recv,
-    early_s, early_r, gather_s, gather_r, tile_s, tile_r, third_s, third_r, unit_s, unit_r, own_s, own_r, far_s, far_r,
+    below_in, early_s, early_r, gather_s, gather_r, tile_s, tile_r, third_s, third_r, unit_s, unit_r, own_s, own_r, far_s, far_r,
     rows_s, rows_r, inner_s, inner_r,
 ):
     b = lax.axis_index("loop")
@@ -37,7 +37,7 @@
     feats = width * n_grp
     part = rows // n_grp
     half = rows // HALVES
-    step = min(256, half)
+    step = half
     n_x = n_grp // 2
     x, y = lax.div(g, 2), lax.rem(g, 2)
 
@@ -55,6 +55,10 @@
 
     def half_of(i):
         return pl.ds(i * half, half)
+
+    def features(c):
+        first = 1 - lax.div(g, n_grp // 2)
+        return pl.ds(pl.multiple_of((first if c == 0 else 1 - first) * (feats // 2), feats // 2), feats // 2)
 
     started = []
 
@@ -73,7 +77,6 @@
         pl.semaphore_signal(barrier, inc=1, device_id=(b, mate(d)), device_id_type=MESH)
     for k in range(1, STEPS):
         pl.semaphore_signal(barrier, inc=1, device_id=block(-k), device_id_type=MESH)
-        pl.semaphore_signal(barrier, inc=1, device_id=block(k), device_id_type=MESH)
 
     tiles[pl.ds(0, part), :] = t_ref[:, 0, :]
     for k in range(1, STEPS - 1):
@@ -96,7 +99,9 @@
     for i in range(HALVES):
         add_squares(g, i, first=True)
 
-    pl.semaphore_wait(barrier, n_grp - 1 + 2 * (STEPS - 1))
+    pl.semaphore_wait(barrier, n_grp - 1 + STEPS - 1)
+    for k in range(1, STEPS):
+        pl.semaphore_signal(below_in, inc=1, device_id=block(k), device_id_type=MESH)
 
     early = [
         send(s_ref.at[part_of(mate(d)), :], rows_raw.at[g], early_s.at[d], early_r.at[d], (b, mate(d)))
@@ -120,14 +125,9 @@
         give(g, i, G_LEFT, right, s_ref)
         give(g, i, G_RIGHT, left, s_ref)
 
-    def send_tile(k):
-        dst = tiles.at[pl.ds(k * part, part), :]
-        return send(sent_tiles.at[k - 1], dst, tile_s.at[k - 1], tile_r.at[k - 1], block(-k))
-
     def urow(k):
         return urows.at[pl.ds(k * part, part), :]
 
-    tile_copies = [send_tile(2), send_tile(1)]
     third_copies = [
         send(third.at[0, mate(d)], third.at[1, g], third_s.at[d], third_r.at[d], (b, mate(d)))
         for d in range(n_grp - 1)
@@ -144,10 +144,6 @@
     rows_norm[...] = norms
     for h in range(n_grp):
         urows[0:part, h * width : (h + 1) * width] = (rows_raw[h].astype(F32) / norms).astype(BF16)
-    unit_copies = [
-        send(urow(0), urow(1), unit_s.at[0], unit_r.at[0], block(-1)),
-        send(urow(0), urow(3), unit_s.at[2], unit_r.at[2], block(3)),
-    ]
 
     def pass_on(i):
         take(G_SIDE, at_x(0, True), i)
@@ -165,11 +161,45 @@
             add_squares(h, i)
 
     pass_on(0)
+    pass_on(1)
+    def copy_to(src, dst, s, r, to):
+        copy = pltpu.make_async_remote_copy(
+            src_ref=src, dst_ref=dst, send_sem=s, recv_sem=r, device_id=to, device_id_type=MESH
+        )
+        started.append(copy)
+        return copy
+
+    def tile_copy(k):
+        dst = tiles.at[pl.ds(k * part, part), :]
+        return copy_to(sent_tiles.at[k - 1], dst, tile_s.at[k - 1], tile_r.at[k - 1], block(-k))
+
+    unit_copies = [
+        copy_to(urow(0), urow(1), unit_s.at[0], unit_r.at[0], block(-1)),
+        copy_to(urow(0), urow(3), unit_s.at[2], unit_r.at[2], block(3)),
+    ]
+    unit_copies[1].start()
+    tile_copies = [tile_copy(2), tile_copy(1)]
+    wrap = lax.rem(b, n_loop // 2) < STEPS - 1
+
+    def send_down():
+        pl.semaphore_wait(below_in, STEPS - 1)
+        unit_copies[0].start()
+        for copy in tile_copies:
+            copy.start()
+
+    @pl.when(jnp.logical_not(wrap))
+    def _():
+        send_down()
+
     use(0, at_x(0, True), at_x(-1))
+    pass_back(0)
+    pass_back(1)
+    @pl.when(wrap)
+    def _():
+        send_down()
+
     unit_copies[0].wait_recv()
     unit_copies.append(send(urow(1), urow(2), unit_s.at[1], unit_r.at[1], block(-1)))
-    pass_on(1)
-    pass_back(0)
     use(0, at_x(1, True))
     take(G_RIGHT, at_x(1), 0)
     take(G_LEFT_SIDE, at_x(-1, True), 0)
@@ -183,7 +213,6 @@
         tiles[3 * part : 4 * part, h * part : (h + 1) * part] = third[1, h].astype(F32).T.astype(BF16)
     take(G_RIGHT_FAR, at_x(2, True), 0)
     use(0, at_x(2, True))
-    pass_back(1)
 
     def normalise(i):
         def piece(j, carry):
@@ -210,18 +239,25 @@
 
         lax.fori_loop(0, half // step, piece, 0)
 
+    def own_parts(i, c):
+        at = features(c)
+        found = jnp.dot(errors[:, half_of(i)], unit[half_of(i), at], preferred_element_type=F32)
+        if i == 0:
+            own_total[c] = found
+        else:
+            found = found + own_total[c]
+            own_total[c, 0:part] = found[:part]
+            for k in range(1, STEPS):
+                own_send[k - 1, c] = found[k * part : (k + 1) * part].astype(BF16)
+
     def far_pair(dx, i):
         pair = lax.rem(x + dx + n_x, n_x)
         mine = urows[:, pl.ds(pl.multiple_of(pair * 2 * width, 2 * width), 2 * width)]
 
-        def piece(j, carry):
-            at = pl.ds(pl.multiple_of(i * half + j * step, step), step)
-            sums = jnp.dot(errors_t[at, :], mine, preferred_element_type=F32).astype(BF16)
-            far[pair * 2, at, :] = sums[:, :width]
-            far[pair * 2 + 1, at, :] = sums[:, width:]
-            return carry
-
-        lax.fori_loop(0, half // step, piece, 0)
+        at = half_of(i)
+        sums = jnp.dot(errors_t[at, :], mine, preferred_element_type=F32).astype(BF16)
+        far[pair * 2, at, :] = sums[:, :width]
+        far[pair * 2 + 1, at, :] = sums[:, width:]
 
     sent_sums = []
 
@@ -235,21 +271,24 @@
         here = landed.at[slot, half_of(i), :]
         pltpu.make_async_copy(here, here, far_r.at[slot, i]).wait()
 
-    def far_terms(i):
+    def far_passes(i):
         far_pair(2, i)
         hand(far.at[at_x(2, True)], i, R_LEFT_PASS, right)
         hand(far.at[at_x(2)], i, R_RIGHT_PASS, left)
-        far_pair(1, i)
-        hand(far.at[at_x(1)], i, R_LEFT, right)
+
+    def far_near(i):
         far_pair(-1, i)
         hand(far.at[at_x(-1, True)], i, R_RIGHT, left)
-        far_pair(0, i)
-
-    def add_passed(i):
+        far_pair(1, i)
+
+    def add_left_pass(i):
         at = half_of(i)
         got(R_LEFT_PASS, i)
         passed[0, at, :] = (far[at_x(1, True), at, :].astype(F32) + landed[R_LEFT_PASS, at, :].astype(F32)).astype(BF16)
         hand(passed.at[0], i, R_LEFT_SUM, right)
+
+    def add_right_pass(i):
+        at = half_of(i)
         got(R_RIGHT_PASS, i)
         passed[1, at, :] = (far[at_x(-1), at, :].astype(F32) + landed[R_RIGHT_PASS, at, :].astype(F32)).astype(BF16)
         hand(passed.at[1], i, R_RIGHT_SUM, left)
@@ -269,7 +308,12 @@
         copy.wait_recv()
     normalise(0)
     error_tiles(0)
-    far_terms(0)
+    far_passes(0)
+    far_near(0)
+    hand(far.at[at_x(1)], 0, R_LEFT, right)
+    far_pair(0, 0)
+    own_parts(0, 0)
+    own_parts(0, 1)
 
     use(1, at_x(1, True))
     take(G_RIGHT, at_x(1), 1)
@@ -280,22 +324,29 @@
     use(1, at_x(-2), at_x(2, True))
     normalise(1)
     error_tiles(1)
-
-    def own_parts(j, carry):
-        at = pl.ds(pl.multiple_of(j * 256, 256), 256)
-        found = jnp.dot(errors[...], unit[:, at], preferred_element_type=F32)
-        own_total[:, at] = found[:part]
-        for k in range(1, STEPS):
-            own_send[k - 1, :, at] = found[k * part : (k + 1) * part].astype(BF16)
-        return carry
-
-    lax.fori_loop(0, feats // 256, own_parts, 0)
-    own_copies = [
-        send(own_send.at[k - 1], own_recv.at[k - 1], own_s.at[k - 1], own_r.at[k - 1], block(k if k < 3 else -3))
-        for k in range(1, STEPS)
-    ]
-    far_terms(1)
-    add_passed(0)
+    own_copies = []
+    for c in range(2):
+        own_parts(1, c)
+        own_copies.append(
+            [
+                send(
+                    own_send.at[k - 1, c],
+                    own_recv.at[k - 1, c],
+                    own_s.at[k - 1, c],
+                    own_r.at[k - 1, c],
+                    block(k if k < 3 else -3),
+                )
+                for k in range(1, STEPS)
+            ]
+        )
+    far_passes(1)
+    add_left_pass(0)
+    add_right_pass(0)
+    far_near(1)
+    add_left_pass(1)
+    hand(far.at[at_x(1)], 1, R_LEFT, right)
+    add_right_pass(1)
+    far_pair(0, 1)
 
     eye = lax.broadcasted_iota(jnp.int32, (part, part), 0) == lax.broadcasted_iota(jnp.int32, (part, part), 1)
 
@@ -308,22 +359,30 @@
         return carry
 
     lax.fori_loop(0, n_grp, inner_rows, 0)
-    add_passed(1)
-
-    for copy in own_copies:
-        copy.wait_recv()
-    total = own_total[...]
-    for k in range(1, STEPS):
-        total = total + own_recv[k - 1].astype(F32)
+    add_side(0)
+
     dots = jnp.zeros((part, width), F32)
-    for h in range(n_grp):
-        rounded = total[:, h * width : (h + 1) * width].astype(BF16)
-        own_rows[h] = rounded
-        dots = dots + rows_raw[h].astype(F32) * rounded.astype(F32)
-    rows_copies = [
-        send(own_rows.at[mate(d)], home_rows.at[part_of(g), :], rows_s.at[d], rows_r.at[d], (b, mate(d)))
-        for d in range(n_grp - 1)
-    ]
+    rows_copies = []
+    near = n_grp // 2
+    mine = lax.div(g, near)
+    for c in range(2):
+        for copy in own_copies[c]:
+            copy.wait_recv()
+        total = own_total[c, 0:part, :]
+        for k in range(1, STEPS):
+            total = total + own_recv[k - 1, c].astype(F32)
+        group = 1 - mine if c == 0 else mine
+        for i in range(near):
+            h = group * near + i
+            rounded = total[:, i * width : (i + 1) * width].astype(BF16)
+            own_rows[h] = rounded
+            dots = dots + rows_raw[h].astype(F32) * rounded.astype(F32)
+        for i in range(near - c):
+            h = group * near + (i if c == 0 else lax.rem(g + 1 + i, near))
+            slot = lax.rem(g - h - 1 + 2 * n_grp, n_grp)
+            rows_copies.append(
+                send(own_rows.at[h], home_rows.at[part_of(g), :], rows_s.at[len(rows_copies)], rows_r.at[slot], (b, h))
+            )
     inner_send[pl.ds(g, 1), :] = inner_send[pl.ds(g, 1), :] + to_lanes(
         jnp.sum(dots, axis=1, keepdims=True) / rows_norm[...], eye
     )
@@ -332,8 +391,7 @@
     ]
     home_rows[part_of(g), :] = own_rows[g]
 
-    for i in range(HALVES):
-        add_side(i)
+    add_side(1)
 
     for copy in rows_copies + inner_copies:
         copy.wait_recv()
@@ -376,23 +434,24 @@
         pltpu.VMEM((2, n_grp, part, part), BF16),
         pltpu.VMEM((STEPS * part, rows), BF16),
         pltpu.VMEM((rows, STEPS * part), BF16),
-        pltpu.VMEM((hops, part, feats), BF16),
-        pltpu.VMEM((hops, part, feats), BF16),
+        pltpu.VMEM((hops, 2, part, feats // 2), BF16),
+        pltpu.VMEM((hops, 2, part, feats // 2), BF16),
         pltpu.VMEM((n_grp, rows, width), BF16),
         pltpu.VMEM((7, rows, width), BF16),
         pltpu.VMEM((2, rows, width), BF16),
         pltpu.VMEM((rows, width), BF16),
-        pltpu.VMEM((part, feats), F32),
+        pltpu.VMEM((2, STEPS * part, feats // 2), F32),
         pltpu.VMEM((n_grp, part, width), BF16),
         pltpu.VMEM((rows, width), BF16),
         pltpu.VMEM((n_grp, part), F32),
         pltpu.VMEM((mates, n_grp, part), F32),
+        pltpu.SemaphoreType.REGULAR,
         dma((mates,)), dma((mates,)),
         dma((7 * HALVES,)), dma((7, HALVES)),
         dma((hops - 1,)), dma((hops - 1,)),
         dma((mates,)), dma((mates,)),
         dma((hops,)), dma((hops,)),
-        dma((hops,)), dma((hops,)),
+        dma((hops, 2)), dma((hops, 2)),
         dma((7 * HALVES,)), dma((7, HALVES)),
         dma((mates,)), dma((mates,)),
         dma((mates,)), dma((mates,)),

time: 81.2 us -> 71.1 us (0.88)
  Pallas kernels: 78.6 us -> 69.1 us
    pallas_call x1, Pallas kernels: 78.6 us -> 69.1 us  [per_device(): pl.pallas_call(functools.partial(kernel, n_loop, n_grp), out_shape=jax.Sh...]
where the time goes in v4:
time: 71.1 us; the launch traced here: 70.9 us
  Pallas kernels  69.1 us (97%)
  local copies, waits for them, and re-layouts  1.87 us (3%)
    pallas_call x1, Pallas kernels, per_device(): pl.pallas_call(functools.partial(kernel, n_loop, n_grp), out_shape=jax.Sh...  69.1 us
    unnamed x1, local copies, waits for them, and re-layouts  1.87 us

profile of v4, /device:TPU:1, one launch (start us, length us, event | category | flops | bytes accessed | tf_op | source)
XLA Modules:
  0.0 70.9 jit_solution(10050614626315915779)
XLA Ops:
  0.0 69.1 %window_grad.1 = f32[1024,128]{1,0:T(8,128)} custom-call(bf16[1024,128]{1,0:T(8,128)(2,1)} %s_ref.1, bf16[128,4,1024]{2,1,0:T(4,128)(2,1)} %t_ref.1), custom_call_target="tpu_custom_call" | custom-call | tf_op jit(solution)/shard_map/window_grad/pallas_call | solution.py:459
  69.1 1.9 %copy.4 = f32[1024,128]{1,0:T(8,128)} copy(f32[1024,128]{1,0:T(8,128)} %window_grad.1) | data formatting | bytes 1048576

commit v5 on v4

--- a/solution.py
+++ b/solution.py
@@ -25,12 +25,19 @@
 
 
 def kernel(
-    n_loop, n_grp, s_ref, t_ref, out_ref,
+    n_loop, n_grp, s_hbm, t_hbm, out_hbm,
+    s_ref, t_ref, out_ref, input_sem, output_sem,
     raw, unit, squares, norm, rows_raw, rows_norm, urows, sent_tiles, tiles, third, errors, errors_t, own_send, own_recv,
     far, landed, passed, side, own_total, own_rows, home_rows, inner_send, inner_recv,
     below_in, early_s, early_r, gather_s, gather_r, tile_s, tile_r, third_s, third_r, unit_s, unit_r, own_s, own_r, far_s, far_r,
     rows_s, rows_r, inner_s, inner_r,
 ):
+    inputs = [
+        pltpu.make_async_copy(s_hbm, s_ref, input_sem.at[0]),
+        pltpu.make_async_copy(t_hbm, t_ref, input_sem.at[1]),
+    ]
+    for copy in inputs:
+        copy.start()
     b = lax.axis_index("loop")
     g = lax.axis_index("grp")
     rows, width = s_ref.shape
@@ -78,6 +85,8 @@
     for k in range(1, STEPS):
         pl.semaphore_signal(barrier, inc=1, device_id=block(-k), device_id_type=MESH)
 
+    for copy in inputs:
+        copy.wait()
     tiles[pl.ds(0, part), :] = t_ref[:, 0, :]
     for k in range(1, STEPS - 1):
         sent_tiles[k - 1] = t_ref[:, k, :]
@@ -132,6 +141,26 @@
         send(third.at[0, mate(d)], third.at[1, g], third_s.at[d], third_r.at[d], (b, mate(d)))
         for d in range(n_grp - 1)
     ]
+    def copy_to(src, dst, s, r, to):
+        copy = pltpu.make_async_remote_copy(
+            src_ref=src, dst_ref=dst, send_sem=s, recv_sem=r, device_id=to, device_id_type=MESH
+        )
+        started.append(copy)
+        return copy
+
+    def tile_copy(k):
+        dst = tiles.at[pl.ds(k * part, part), :]
+        return copy_to(sent_tiles.at[k - 1], dst, tile_s.at[k - 1], tile_r.at[k - 1], block(-k))
+
+    tile_copies = [tile_copy(2), tile_copy(1)]
+    wrap = lax.rem(b, n_loop // 2) < STEPS - 1
+
+    @pl.when(jnp.logical_not(wrap))
+    def _():
+        pl.semaphore_wait(below_in, STEPS - 1)
+        for copy in tile_copies:
+            copy.start()
+
     third[1, g] = third[0, g]
 
     for copy in early:
@@ -145,6 +174,16 @@
     for h in range(n_grp):
         urows[0:part, h * width : (h + 1) * width] = (rows_raw[h].astype(F32) / norms).astype(BF16)
 
+    unit_copies = [
+        copy_to(urow(0), urow(1), unit_s.at[0], unit_r.at[0], block(-1)),
+        copy_to(urow(0), urow(3), unit_s.at[2], unit_r.at[2], block(3)),
+    ]
+    unit_copies[1].start()
+
+    @pl.when(jnp.logical_not(wrap))
+    def _():
+        unit_copies[0].start()
+
     def pass_on(i):
         take(G_SIDE, at_x(0, True), i)
         give(at_x(0, True), i, G_LEFT_SIDE, right)
@@ -162,44 +201,30 @@
 
     pass_on(0)
     pass_on(1)
-    def copy_to(src, dst, s, r, to):
-        copy = pltpu.make_async_remote_copy(
-            src_ref=src, dst_ref=dst, send_sem=s, recv_sem=r, device_id=to, device_id_type=MESH
-        )
-        started.append(copy)
-        return copy
-
-    def tile_copy(k):
-        dst = tiles.at[pl.ds(k * part, part), :]
-        return copy_to(sent_tiles.at[k - 1], dst, tile_s.at[k - 1], tile_r.at[k - 1], block(-k))
-
-    unit_copies = [
-        copy_to(urow(0), urow(1), unit_s.at[0], unit_r.at[0], block(-1)),
-        copy_to(urow(0), urow(3), unit_s.at[2], unit_r.at[2], block(3)),
-    ]
-    unit_copies[1].start()
-    tile_copies = [tile_copy(2), tile_copy(1)]
-    wrap = lax.rem(b, n_loop // 2) < STEPS - 1
-
-    def send_down():
-        pl.semaphore_wait(below_in, STEPS - 1)
-        unit_copies[0].start()
-        for copy in tile_copies:
-            copy.start()
+    unit_copies.append(copy_to(urow(1), urow(2), unit_s.at[1], unit_r.at[1], block(-1)))
+
+    def relay():
+        unit_copies[0].wait_recv()
+        unit_copies[2].start()
 
     @pl.when(jnp.logical_not(wrap))
     def _():
-        send_down()
+        relay()
 
     use(0, at_x(0, True), at_x(-1))
     pass_back(0)
     pass_back(1)
     @pl.when(wrap)
     def _():
-        send_down()
-
-    unit_copies[0].wait_recv()
-    unit_copies.append(send(urow(1), urow(2), unit_s.at[1], unit_r.at[1], block(-1)))
+        pl.semaphore_wait(below_in, STEPS - 1)
+        unit_copies[0].start()
+        for copy in tile_copies:
+            copy.start()
+
+    @pl.when(wrap)
+    def _():
+        relay()
+
     use(0, at_x(1, True))
     take(G_RIGHT, at_x(1), 0)
     take(G_LEFT_SIDE, at_x(-1, True), 0)
@@ -393,26 +418,41 @@
 
     add_side(1)
 
+    def add_home(i):
+        for slot in (R_LEFT, R_RIGHT_SUM, R_SIDE):
+            got(slot, i)
+        at = half_of(i)
+        grad = far[g, at, :].astype(F32)
+        for slot in (R_LEFT, R_RIGHT_SUM, R_SIDE):
+            grad = grad + landed[slot, at, :].astype(F32)
+        out_ref[at, :] = grad
+
+    add_home(0)
     for copy in rows_copies + inner_copies:
         copy.wait_recv()
     inner = inner_send[...]
     for d in range(n_grp - 1):
         inner = inner + inner_recv[d]
 
-    for i in range(n_grp):
-        if i % (n_grp // HALVES) == 0:
-            for slot in (R_LEFT, R_RIGHT_SUM, R_SIDE):
-                got(slot, i // (n_grp // HALVES))
-        at = pl.ds(i * part, part)
-        grad = home_rows[at, :].astype(F32) + far[g, at, :].astype(F32)
-        for slot in (R_LEFT, R_RIGHT_SUM, R_SIDE):
-            grad = grad + landed[slot, at, :].astype(F32)
-        inverse = 1.0 / norm[at, :]
-        along = to_column(inner[i : i + 1, :], eye)
-        out_ref[at, :] = (2.0 * inverse) * (grad - s_ref[at, :].astype(F32) * (inverse * along))
+    outputs = []
+    for i in range(HALVES):
+        if i > 0:
+            add_home(i)
+        for j in range(i * n_grp // HALVES, (i + 1) * n_grp // HALVES):
+            at = pl.ds(j * part, part)
+            grad = home_rows[at, :].astype(F32) + out_ref[at, :]
+            inverse = 1.0 / norm[at, :]
+            along = to_column(inner[j : j + 1, :], eye)
+            out_ref[at, :] = (2.0 * inverse) * (grad - s_ref[at, :].astype(F32) * (inverse * along))
+        outputs.append(
+            pltpu.make_async_copy(out_ref.at[half_of(i), :], out_hbm.at[half_of(i), :], output_sem.at[i])
+        )
+        outputs[i].start()
 
     for copy in started:
         copy.wait_send()
+    for copy in outputs:
+        copy.wait()
 
 
 def per_device(n_loop, n_grp, student, teacher_tiles):
@@ -422,6 +462,11 @@
     mates, hops = n_grp - 1, STEPS - 1
     dma = pltpu.SemaphoreType.DMA
     scratch = [
+        pltpu.VMEM((rows, width), BF16),
+        pltpu.VMEM((part, STEPS, rows), BF16),
+        pltpu.VMEM((rows, width), F32),
+        dma((2,)),
+        dma((HALVES,)),
         pltpu.VMEM((n_grp, rows, width), BF16),
         pltpu.VMEM((rows, feats), BF16),
         pltpu.VMEM((rows, width), F32),
@@ -459,8 +504,8 @@
     return pl.pallas_call(
         functools.partial(kernel, n_loop, n_grp),
         out_shape=jax.ShapeDtypeStruct((rows, width), F32),
-        in_specs=[pl.BlockSpec(memory_space=pltpu.VMEM)] * 2,
-        out_specs=pl.BlockSpec(memory_space=pltpu.VMEM),
+        in_specs=[pl.BlockSpec(memory_space=pl.ANY)] * 2,
+        out_specs=pl.BlockSpec(memory_space=pl.ANY),
         scratch_shapes=scratch,
         compiler_params=pltpu.CompilerParams(
             collective_id=0, has_side_effects=True, vmem_limit_bytes=56 * 2**20

time: 71.1 us -> 70 us (0.985)
  Pallas kernels: 69.1 us -> 68 us
    pallas_call x1, Pallas kernels: 69.1 us -> 68 us  [per_device(): pl.pallas_call(functools.partial(kernel, n_loop, n_grp), out_shape=jax.Sh...]
where the time goes in v5:
time: 70 us; the launch traced here: 69.8 us
  Pallas kernels  68 us (97%)
  local copies, waits for them, and re-layouts  1.87 us (3%)
    pallas_call x1, Pallas kernels, per_device(): pl.pallas_call(functools.partial(kernel, n_loop, n_grp), out_shape=jax.Sh...  68 us
    unnamed x1, local copies, waits for them, and re-layouts  1.87 us

profile of v5, /device:TPU:1, one launch (start us, length us, event | category | flops | bytes accessed | tf_op | source)
XLA Modules:
  0.0 69.8 jit_solution(16257385158263512649)
XLA Ops:
  0.0 68.0 %window_grad.1 = f32[1024,128]{1,0:T(8,128)} custom-call(bf16[1024,128]{1,0:T(8,128)(2,1)} %s_hbm.1, bf16[128,4,1024]{2,1,0:T(4,128)(2,1)} %t_hbm.1), custom_call_target="tpu_custom_call" | custom-call | tf_op jit(solution)/shard_map/window_grad/pallas_call | solution.py:504
  68.0 1.9 %copy.4 = f32[1024,128]{1,0:T(8,128)} copy(f32[1024,128]{1,0:T(8,128)} %window_grad.1) | data formatting | bytes 1048576

commit v6 on v5

--- a/solution.py
+++ b/solution.py
@@ -264,16 +264,11 @@
 
         lax.fori_loop(0, half // step, piece, 0)
 
-    def own_parts(i, c):
-        at = features(c)
-        found = jnp.dot(errors[:, half_of(i)], unit[half_of(i), at], preferred_element_type=F32)
-        if i == 0:
-            own_total[c] = found
-        else:
-            found = found + own_total[c]
-            own_total[c, 0:part] = found[:part]
-            for k in range(1, STEPS):
-                own_send[k - 1, c] = found[k * part : (k + 1) * part].astype(BF16)
+    def own_parts(c):
+        found = jnp.dot(errors[...], unit[:, features(c)], preferred_element_type=F32)
+        own_total[c] = found[:part]
+        for k in range(1, STEPS):
+            own_send[k - 1, c] = found[k * part : (k + 1) * part].astype(BF16)
 
     def far_pair(dx, i):
         pair = lax.rem(x + dx + n_x, n_x)
@@ -336,9 +331,6 @@
     far_passes(0)
     far_near(0)
     hand(far.at[at_x(1)], 0, R_LEFT, right)
-    far_pair(0, 0)
-    own_parts(0, 0)
-    own_parts(0, 1)
 
     use(1, at_x(1, True))
     take(G_RIGHT, at_x(1), 1)
@@ -351,7 +343,7 @@
     error_tiles(1)
     own_copies = []
     for c in range(2):
-        own_parts(1, c)
+        own_parts(c)
         own_copies.append(
             [
                 send(
@@ -371,6 +363,7 @@
     add_left_pass(1)
     hand(far.at[at_x(1)], 1, R_LEFT, right)
     add_right_pass(1)
+    far_pair(0, 0)
     far_pair(0, 1)
 
     eye = lax.broadcasted_iota(jnp.int32, (part, part), 0) == lax.broadcasted_iota(jnp.int32, (part, part), 1)
@@ -393,7 +386,7 @@
     for c in range(2):
         for copy in own_copies[c]:
             copy.wait_recv()
-        total = own_total[c, 0:part, :]
+        total = own_total[c]
         for k in range(1, STEPS):
             total = total + own_recv[k - 1, c].astype(F32)
         group = 1 - mine if c == 0 else mine
@@ -485,7 +478,7 @@
         pltpu.VMEM((7, rows, width), BF16),
         pltpu.VMEM((2, rows, width), BF16),
         pltpu.VMEM((rows, width), BF16),
-        pltpu.VMEM((2, STEPS * part, feats // 2), F32),
+        pltpu.VMEM((2, part, feats // 2), F32),
         pltpu.VMEM((n_grp, part, width), BF16),
         pltpu.VMEM((rows, width), BF16),
         pltpu.VMEM((n_grp, part), F32),

time: 70 us -> 69.3 us (0.990)
  Pallas kernels: 68 us -> 67.3 us
where the time goes in v6:
time: 69.3 us; the launch traced here: 69.2 us
  Pallas kernels  67.3 us (97%)
  local copies, waits for them, and re-layouts  1.87 us (3%)
    pallas_call x1, Pallas kernels, per_device(): pl.pallas_call(functools.partial(kernel, n_loop, n_grp), out_shape=jax.Sh...  67.3 us
    unnamed x1, local copies, waits for them, and re-layouts  1.87 us

profile of v6, /device:TPU:1, one launch (start us, length us, event | category | flops | bytes accessed | tf_op | source)
XLA Modules:
  0.0 69.2 jit_solution(10631554451696902745)
XLA Ops:
  0.0 67.3 %window_grad.1 = f32[1024,128]{1,0:T(8,128)} custom-call(bf16[1024,128]{1,0:T(8,128)(2,1)} %s_hbm.1, bf16[128,4,1024]{2,1,0:T(4,128)(2,1)} %t_hbm.1), custom_call_target="tpu_custom_call" | custom-call | tf_op jit(solution)/shard_map/window_grad/pallas_call | solution.py:497
  67.3 1.9 %copy.4 = f32[1024,128]{1,0:T(8,128)} copy(f32[1024,128]{1,0:T(8,128)} %window_grad.1) | data formatting | bytes 1048576

commit v7 on v6

--- a/solution.py
+++ b/solution.py
@@ -394,13 +394,14 @@
             h = group * near + i
             rounded = total[:, i * width : (i + 1) * width].astype(BF16)
             own_rows[h] = rounded
-            dots = dots + rows_raw[h].astype(F32) * rounded.astype(F32)
         for i in range(near - c):
             h = group * near + (i if c == 0 else lax.rem(g + 1 + i, near))
             slot = lax.rem(g - h - 1 + 2 * n_grp, n_grp)
             rows_copies.append(
                 send(own_rows.at[h], home_rows.at[part_of(g), :], rows_s.at[len(rows_copies)], rows_r.at[slot], (b, h))
             )
+    for h in range(n_grp):
+        dots = dots + rows_raw[h].astype(F32) * own_rows[h].astype(F32)
     inner_send[pl.ds(g, 1), :] = inner_send[pl.ds(g, 1), :] + to_lanes(
         jnp.sum(dots, axis=1, keepdims=True) / rows_norm[...], eye
     )

time: 69.3 us -> 69.3 us (level)
  no operation moved by 1% of the time
where the time goes in v7:
time: 69.3 us; the launch traced here: 69.1 us
  Pallas kernels  67.3 us (97%)
  local copies, waits for them, and re-layouts  1.87 us (3%)
    pallas_call x1, Pallas kernels, per_device(): pl.pallas_call(functools.partial(kernel, n_loop, n_grp), out_shape=jax.Sh...  67.3 us
    unnamed x1, local copies, waits for them, and re-layouts  1.87 us

profile of v7, /device:TPU:1, one launch (start us, length us, event | category | flops | bytes accessed | tf_op | source)
XLA Modules:
  0.0 69.1 jit_solution(2381109977965371142)
XLA Ops:
  0.0 67.3 %window_grad.1 = f32[1024,128]{1,0:T(8,128)} custom-call(bf16[1024,128]{1,0:T(8,128)(2,1)} %s_hbm.1, bf16[128,4,1024]{2,1,0:T(4,128)(2,1)} %t_hbm.1), custom_call_target="tpu_custom_call" | custom-call | tf_op jit(solution)/shard_map/window_grad/pallas_call | solution.py:498
  67.3 1.9 %copy.4 = f32[1024,128]{1,0:T(8,128)} copy(f32[1024,128]{1,0:T(8,128)} %window_grad.1) | data formatting | bytes 1048576
